TPU v7x, 1024 devices: a whole 8x8x8 slice. The times are simulated.
1024 devices in a mesh: lon: 64 (over x, y), lat: 16 (over z, core).
Axes of the slice: x: 8, y: 8, z: 8, core: 2. Of those that a mesh axis runs over, the one named last changes fastest.
Arguments:
- grid_latent: bfloat16 [256, 2048, 512], P('lat', 'lon'), may hold values from -6 to 6
- mesh_latent: bfloat16 [16, 64, 40, 512], P('lat', 'lon'), may hold values from -6 to 6
- grid_senders: int32 [16, 64, 1024], P('lat', 'lon'), may hold values from 0 to 835, as said below
- grid_targets: int32 [16, 64, 1024], P('lat', 'lon'), may hold values from 0 to 39
- grid_geometry: bfloat16 [16, 64, 4, 1024], P('lat', 'lon'), may hold values from -6 to 6
- mesh_senders: int32 [16, 64, 512], P('lat', 'lon'), may hold values from 0 to 1383, as said below
- mesh_targets: int32 [16, 64, 512], P('lat', 'lon'), may hold values from 0 to 39
- mesh_geometry: bfloat16 [16, 64, 4, 512], P('lat', 'lon'), may hold values from -6 to 6
- edge_counts: int32 [2, 16, 64], P(None, 'lat', 'lon'), may hold values from 128 to 1024, as said below
- encode_sender: bfloat16 [512, 512], replicated, may hold values from -0.25 to 0.25
- encode_target: bfloat16 [512, 512], replicated, may hold values from -0.25 to 0.25
- encode_geometry: bfloat16 [4, 512], replicated, may hold values from -3 to 3
- encode_output: bfloat16 [512, 512], replicated, may hold values from -0.25 to 0.25
- encode_self: bfloat16 [512, 512], replicated, may hold values from -0.25 to 0.25
- encode_inflow: bfloat16 [512, 512], replicated, may hold values from -0.25 to 0.25
- encode_final: bfloat16 [512, 512], replicated, may hold values from -0.25 to 0.25
- process_sender: bfloat16 [512, 512], replicated, may hold values from -1 to 1
- process_target: bfloat16 [512, 512], replicated, may hold values from -0.25 to 0.25
- process_geometry: bfloat16 [4, 512], replicated, may hold values from -3 to 3
- process_output: bfloat16 [512, 512], replicated, may hold values from -0.25 to 0.25
- process_self: bfloat16 [512, 512], replicated, may hold values from -0.25 to 0.25
- process_inflow: bfloat16 [512, 512], replicated, may hold values from -0.25 to 0.25
- process_final: bfloat16 [512, 512], replicated, may hold values from -0.25 to 0.25
Outputs:
- processed: bfloat16 [16, 64, 40, 512], P('lat', 'lon')
Inputs may be any that keep to these rules, and one draw needn't show every extreme that they name: `grid_senders`: never names a grid row outside the grid: band 0 uses no r below 3, the last band no r at or above 19. `mesh_senders`: never names a neighbouring sector outside the latitude bands. `edge_counts`: multiples of 128, at least 128 and at most 1024 in row 0 and 512 in row 1; each row's capacity is reached by some sector in every draw.
All inputs are finite; a program needn't handle non-finite values.
Results may differ from a plain program's by a relative error of at most 0.013.
Values may be sent and summed in bfloat16 or wider, within the bound.
A program may use at most 32 MiB of HBM per device.

v0:
```python
import jax
import jax.numpy as jnp
from jax import lax
from jax.sharding import PartitionSpec as P

RIM_CELLS = 3


def padded(shard, sides, width):
    for axis, dim in sides:
        devices, length = (lax.axis_size(axis), shard.shape[dim])
        up = [(i, (i + 1) % devices) for i in range(devices)]
        down = [(j, i) for i, j in up]
        last = lax.slice_in_dim(shard, length - width, length, axis=dim)
        first = lax.slice_in_dim(shard, 0, width, axis=dim)
        before = lax.ppermute(last, axis, up)
        after = lax.ppermute(first, axis, down)
        shard = jnp.concatenate([before, shard, after], axis=dim)
    return shard


def layer_norm(values):
    centre = jnp.mean(values, axis=-1, keepdims=True)
    shifted = values - centre
    spread = jnp.mean(shifted * shifted, axis=-1, keepdims=True)
    return shifted * lax.rsqrt(spread + 1e-05)


def project(latent, weight):
    return jnp.dot(latent, weight, preferred_element_type=jnp.float32).astype(jnp.bfloat16)


def edge_update(
    sender_part,
    targets,
    geometry,
    live_count,
    mesh_nodes,
    w_target,
    w_geometry,
    w_output,
    w_self,
    w_inflow,
    w_final,
):
    edge_total = targets.shape[0]
    slot_count = mesh_nodes.shape[0]
    incidence = (targets[None, :] == jnp.arange(slot_count, dtype=jnp.int32)[:, None]).astype(
        jnp.float32
    )
    target_term = jnp.dot(mesh_nodes, w_target, preferred_element_type=jnp.float32)
    target_rows = lax.dot_general(
        incidence,
        target_term,
        (((0,), (0,)), ((), ())),
        precision=lax.Precision.HIGHEST,
        preferred_element_type=jnp.float32,
    )
    geometry_term = lax.dot_general(
        geometry, w_geometry, (((0,), (0,)), ((), ())), preferred_element_type=jnp.float32
    )
    hidden = jax.nn.silu(geometry_term + sender_part.astype(jnp.float32) + target_rows).astype(
        jnp.bfloat16
    )
    message = layer_norm(jnp.dot(hidden, w_output, preferred_element_type=jnp.float32))
    is_live = jnp.arange(edge_total, dtype=jnp.int32) < live_count
    message = jnp.where(is_live[:, None], message, 0.0)
    inflow = jnp.dot(
        incidence, message, precision=lax.Precision.HIGHEST, preferred_element_type=jnp.float32
    ).astype(jnp.bfloat16)
    inner_sum = jnp.dot(mesh_nodes, w_self, preferred_element_type=jnp.float32)
    inner_sum = inner_sum + jnp.dot(inflow, w_inflow, preferred_element_type=jnp.float32)
    inner_hidden = jax.nn.silu(inner_sum).astype(jnp.bfloat16)
    update = layer_norm(jnp.dot(inner_hidden, w_final, preferred_element_type=jnp.float32))
    return (mesh_nodes.astype(jnp.float32) + update).astype(jnp.bfloat16)


def body(
    grid_latent,
    mesh_latent,
    grid_senders,
    grid_targets,
    grid_geometry,
    mesh_senders,
    mesh_targets,
    mesh_geometry,
    edge_counts,
    encode_sender,
    encode_target,
    encode_geometry,
    encode_output,
    encode_self,
    encode_inflow,
    encode_final,
    process_sender,
    process_target,
    process_geometry,
    process_output,
    process_self,
    process_inflow,
    process_final,
):
    lat_rows, lon_cols, latent_width = grid_latent.shape
    mesh_nodes = mesh_latent[0, 0]
    slot_count = mesh_nodes.shape[0]
    extended = padded(grid_latent, (("lon", 1), ("lat", 0)), RIM_CELLS)
    grid_rows = jnp.take(extended.reshape(-1, latent_width), grid_senders[0, 0], axis=0)
    grid_part = project(grid_rows, encode_sender)
    encoded = edge_update(
        grid_part,
        grid_targets[0, 0],
        grid_geometry[0, 0],
        edge_counts[0, 0, 0],
        mesh_nodes,
        encode_target,
        encode_geometry,
        encode_output,
        encode_self,
        encode_inflow,
        encode_final,
    )
    nearby = padded(encoded[None, None], (("lon", 1), ("lat", 0)), 1)
    coarse = lax.all_gather(encoded[0:1], ("lon", "lat"), axis=0, tiled=True)
    source_table = jnp.concatenate([nearby.reshape(9 * slot_count, latent_width), coarse], axis=0)
    mesh_rows = jnp.take(source_table, mesh_senders[0, 0], axis=0)
    mesh_part = project(mesh_rows, process_sender)
    processed = edge_update(
        mesh_part,
        mesh_targets[0, 0],
        mesh_geometry[0, 0],
        edge_counts[1, 0, 0],
        encoded,
        process_target,
        process_geometry,
        process_output,
        process_self,
        process_inflow,
        process_final,
    )
    return processed[None, None]


def solution(mesh):
    return jax.shard_map(
        body,
        mesh=mesh,
        in_specs=(
            P("lat", "lon", None),
            P("lat", "lon", None, None),
            P("lat", "lon", None),
            P("lat", "lon", None),
            P("lat", "lon", None, None),
            P("lat", "lon", None),
            P("lat", "lon", None),
            P("lat", "lon", None, None),
            P(None, "lat", "lon"),
            P(),
            P(),
            P(),
            P(),
            P(),
            P(),
            P(),
            P(),
            P(),
            P(),
            P(),
            P(),
            P(),
            P(),
        ),
        out_specs=P("lat", "lon", None, None),
        check_vma=False,
    )
```

profile of v0, /device:TPU:1, one launch (start us, length us, event | category | flops | bytes accessed | tf_op | source)
XLA Modules:
  0.0 192.2 jit_solution(13477413172620258213)
XLA Ops:
  6.5 1.1 fusion.47
  7.7 4.1 %collective-permute-start = (bf16[16,3,512]{2,1,0:T(4,128)(2,1)S(1)}, bf16[16,3,512]{2,1,0:T(4,128)(2,1)S(1)}, u32[]{:S(2)}, u32[]{:S(2)}) collective-permute-start(bf16[16,3,512]{2,1,0:T(4,128)(2,1)S(1)} %get-tuple-element.7), channel_id=1, source_target_pairs={{0,16},{16,32},{32,48},{48,64},{64,80},{80,96},{96,112},{112,128},... | collective-permute-start | bytes 147464 | tf_op jit(solution)/shard_map/ppermute | solution.py:16
  11.8 6.8 %collective-permute-start.1 = (bf16[16,3,512]{2,1,0:T(4,128)(2,1)S(1)}, bf16[16,3,512]{2,1,0:T(4,128)(2,1)S(1)}, u32[]{:S(2)}, u32[]{:S(2)}) collective-permute-start(bf16[16,3,512]{2,1,0:T(4,128)(2,1)S(1)} %get-tuple-element.8), channel_id=1, source_target_pairs={{16,0},{32,16},{48,32},{64,48},{80,64},{96,80},{112,96},{128,112},... | collective-permute-start | bytes 147464 | tf_op jit(solution)/shard_map/ppermute | solution.py:17
  18.6 0.7 compare_select_fusion
  19.3 1.3 fusion.30
  20.6 1.3 fusion.32
  21.9 2.5 %fusion.38 = f32[1024,512]{1,0:T(8,128)} fusion(bf16[4,512]{1,0:T(4,128)(2,1)} %param.34, bf16[1,1,4,1024]{3,2,1,0:T(4,128)(2,1)} %param.27), kind=kOutput, calls=%fused_computation.68 | convolution fusion | flops 4194304 | bytes 2109440 | tf_op jit(solution)/shard_map/dot_general | solution.py:59
  24.6 3.9 %collective-permute-start.2 = (bf16[3,38,512]{2,1,0:T(8,128)(2,1)S(1)}, bf16[3,38,512]{2,1,0:T(8,128)(2,1)S(1)}, u32[]{:S(2)}, u32[]{:S(2)}) collective-permute-start(bf16[3,38,512]{2,1,0:T(8,128)(2,1)S(1)} %get-tuple-element.5), channel_id=1, source_target_pairs={{0,1},{1,2},{2,3},{3,4},{4,5},{5,6},{6,7},{7,8},{8,9},{9,10},{10,1... | collective-permute-start | bytes 350216 | tf_op jit(solution)/shard_map/ppermute | solution.py:16
  28.4 8.5 %collective-permute-start.3 = (bf16[3,38,512]{2,1,0:T(8,128)(2,1)S(1)}, bf16[3,38,512]{2,1,0:T(8,128)(2,1)S(1)}, u32[]{:S(2)}, u32[]{:S(2)}) collective-permute-start(bf16[3,38,512]{2,1,0:T(8,128)(2,1)S(1)} %get-tuple-element.6), channel_id=1, source_target_pairs={{1,0},{2,1},{3,2},{4,3},{5,4},{6,5},{7,6},{8,7},{9,8},{10,9},{11,1... | collective-permute-start | bytes 350216 | tf_op jit(solution)/shard_map/ppermute | solution.py:17
  37.0 0.6 fusion.48
  37.6 0.6 iota_compare_fusion.6
  38.8 4.0 %gather_fusion = bf16[1024,512]{1,0:T(8,128)(2,1)S(1)} fusion(bf16[836,512]{1,0:T(8,128)(2,1)S(1)} %reshape.132, s32[1024]{0:T(1024)S(1)} %broadcast_clamp_fusion), kind=kCustom, calls=%fused_computation | custom fusion | bytes 2101248 | tf_op jit(solution)/shard_map/jit(_take)/gather | solution.py:107
  42.8 0.8 convolution_convert_fusion
  43.6 0.8 copy-done.2
  44.4 1.6 multiply_convert_fusion
  46.0 0.8 fusion.49
  47.2 1.3 fusion.5
  49.3 0.6 slice_bitcast_fusion
  49.9 0.6 iota_compare_fusion.7
  50.6 3.4 %collective-permute-start.5 = (bf16[1,1,40,512]{3,2,1,0:T(8,128)(2,1)S(1)}, bf16[1,1,40,512]{3,2,1,0:T(8,128)(2,1)S(1)}, u32[]{:S(2)}, u32[]{:S(2)}) collective-permute-start(bf16[1,1,40,512]{3,2,1,0:T(8,128)(2,1)S(1)} %bitcast.56), channel_id=1, source_target_pairs={{16,0},{32,16},{48,32},{64,48},{80,64},{96,80},{112,96},{128,112},... | collective-permute-start | bytes 122888 | tf_op jit(solution)/shard_map/ppermute | solution.py:17
  54.0 1.9 collective-permute-start.4
  56.1 5.9 %collective-permute-done.4 = bf16[1,1,40,512]{3,2,1,0:T(8,128)(2,1)S(1)} collective-permute-done((bf16[1,1,40,512]{3,2,1,0:T(8,128)(2,1)S(1)}, bf16[1,1,40,512]{3,2,1,0:T(8,128)(2,1)S(1)}, u32[]{:S(2)}, u32[]{:S(2)}) %collective-permute-start.4) | collective-permute-done | bytes 40992 | tf_op jit(solution)/shard_map/ppermute | solution.py:16
  62.1 5.8 %collective-permute-start.7 = (bf16[1,3,40,512]{3,2,1,0:T(8,128)(2,1)S(1)}, bf16[1,3,40,512]{3,2,1,0:T(8,128)(2,1)S(1)}, u32[]{:S(2)}, u32[]{:S(2)}) collective-permute-start(bf16[1,3,40,512]{3,2,1,0:T(8,128)(2,1)S(1)} %pad_maximum_fusion.6), channel_id=1, source_target_pairs={{1,0},{2,1},{3,2},{4,3},{5,4},{6,5},{7,6},{8,7},{9,8},{10,9},{11,1... | collective-permute-start | bytes 368648 | tf_op jit(solution)/shard_map/ppermute | solution.py:17
  68.1 0.8 collective-permute-done.7
  68.9 1.4 collective-permute-done.6
  70.3 106.1 %all-gather.3.cloned.1.call-done = bf16[1024,1,512]{2,1,0:T(2,128)(2,1)} async-done(((bf16[1,1,512]{2,1,0:T(2,128)(2,1)}), bf16[1024,1,512]{2,1,0:T(2,128)(2,1)}) %all-gather.3.cloned.1.call-update) | async-done | bytes 1048592 | tf_op jit(solution)/shard_map/all_gather | solution.py:123
  176.4 1.9 copy.26
  178.4 2.0 %gather_fusion.1 = bf16[512,512]{1,0:T(8,128)(2,1)S(1)} fusion(bf16[1384,512]{1,0:T(8,128)(2,1)S(1)} %pad_maximum_fusion, s32[1024]{0:T(1024)S(1)} %pad_clamp_fusion), kind=kCustom, calls=%fused_computation.1 | custom fusion | bytes 1050624 | tf_op jit(solution)/shard_map/jit(_take)/gather | solution.py:125
  181.5 0.8 multiply_convert_fusion.1
  182.5 0.5 fusion.51
  183.2 0.7 convolution_convert_fusion.2
  184.7 0.7 fusion.29
  (77 shorter events, 4.5 us)
Async XLA Ops:
  6.5 39.4 %copy-start = (bf16[512,512]{1,0:T(8,128)(2,1)S(1)}, bf16[512,512]{1,0:T(8,128)(2,1)}, u32[]{:S(2)}) copy-start(bf16[512,512]{1,0:T(8,128)(2,1)} %param.35) | copy-start | bytes 1572868
  6.5 17.9 %copy-start.1 = (bf16[16,32,512]{2,1,0:T(8,128)(2,1)S(1)}, bf16[16,32,512]{2,1,0:T(8,128)(2,1)}, u32[]{:S(2)}) copy-start(bf16[16,32,512]{2,1,0:T(8,128)(2,1)} %param.23) | copy-start | bytes 1572868
  6.5 17.9 %copy-start.12 = (s32[1,1,1024]{2,1,0:T(1,128)S(1)}, s32[1,1,1024]{2,1,0:T(1,128)}, u32[]{:S(2)}) copy-start(s32[1,1,1024]{2,1,0:T(1,128)} %param.25) | copy-start | bytes 12292
  6.5 169.9 %all-gather.3.cloned.1.call-start = ((), (), s32[]{:S(2)}) async-start(), calls=%async_computation | async-start | bytes 2099200 | tf_op jit(solution)/shard_map/all_gather | solution.py:123
  7.7 16.8 %collective-permute-start = (bf16[16,3,512]{2,1,0:T(4,128)(2,1)S(1)}, bf16[16,3,512]{2,1,0:T(4,128)(2,1)S(1)}, u32[]{:S(2)}, u32[]{:S(2)}) collective-permute-start(bf16[16,3,512]{2,1,0:T(4,128)(2,1)S(1)} %get-tuple-element.7), channel_id=1, source_target_pairs={{0,16},{16,32},{32,48},{48,64},{64,80},{80,96},{96,112},{112,128},... | collective-permute-start | bytes 147464 | tf_op jit(solution)/shard_map/ppermute | solution.py:16
  11.8 12.6 %collective-permute-start.1 = (bf16[16,3,512]{2,1,0:T(4,128)(2,1)S(1)}, bf16[16,3,512]{2,1,0:T(4,128)(2,1)S(1)}, u32[]{:S(2)}, u32[]{:S(2)}) collective-permute-start(bf16[16,3,512]{2,1,0:T(4,128)(2,1)S(1)} %get-tuple-element.8), channel_id=1, source_target_pairs={{16,0},{32,16},{48,32},{64,48},{80,64},{96,80},{112,96},{128,112},... | collective-permute-start | bytes 147464 | tf_op jit(solution)/shard_map/ppermute | solution.py:17
  19.3 17.6 %copy-start.17 = (s32[2,1,1]{0,2,1:T(1,128)S(1)}, s32[2,1,1]{0,2,1:T(1,128)}, u32[]{:S(2)}) copy-start(s32[2,1,1]{0,2,1:T(1,128)} %param.31) | copy-start | bytes 28
  24.6 13.7 %collective-permute-start.2 = (bf16[3,38,512]{2,1,0:T(8,128)(2,1)S(1)}, bf16[3,38,512]{2,1,0:T(8,128)(2,1)S(1)}, u32[]{:S(2)}, u32[]{:S(2)}) collective-permute-start(bf16[3,38,512]{2,1,0:T(8,128)(2,1)S(1)} %get-tuple-element.5), channel_id=1, source_target_pairs={{0,1},{1,2},{2,3},{3,4},{4,5},{5,6},{6,7},{7,8},{8,9},{9,10},{10,1... | collective-permute-start | bytes 350216 | tf_op jit(solution)/shard_map/ppermute | solution.py:16
  28.4 9.8 %collective-permute-start.3 = (bf16[3,38,512]{2,1,0:T(8,128)(2,1)S(1)}, bf16[3,38,512]{2,1,0:T(8,128)(2,1)S(1)}, u32[]{:S(2)}, u32[]{:S(2)}) collective-permute-start(bf16[3,38,512]{2,1,0:T(8,128)(2,1)S(1)} %get-tuple-element.6), channel_id=1, source_target_pairs={{1,0},{2,1},{3,2},{4,3},{5,4},{6,5},{7,6},{8,7},{9,8},{10,9},{11,1... | collective-permute-start | bytes 350216 | tf_op jit(solution)/shard_map/ppermute | solution.py:17
  38.8 4.0 %copy-start.18 = (bf16[512,512]{1,0:T(8,128)(2,1)S(1)}, bf16[512,512]{1,0:T(8,128)(2,1)}, u32[]{:S(2)}) copy-start(bf16[512,512]{1,0:T(8,128)(2,1)} %param.32) | copy-start | bytes 1572868
  42.8 1.6 copy-start.2
  42.8 1.6 copy-start.19
  46.8 1.7 copy-start.7
  46.8 1.7 copy-start.8
  47.1 2.1 %copy-start.11 = (bf16[1,1,40,512]{3,2,1,0:T(8,128)(2,1)S(1)}, bf16[1,1,40,512]{3,2,1,0:T(8,128)(2,1)}, u32[]{:S(2)}) copy-start(bf16[1,1,40,512]{3,2,1,0:T(8,128)(2,1)} %param.24) | copy-start | bytes 122884
  47.1 3.4 %copy-start.13 = (s32[1,1,512]{2,1,0:T(1,128)S(1)}, s32[1,1,512]{2,1,0:T(1,128)}, u32[]{:S(2)}) copy-start(s32[1,1,512]{2,1,0:T(1,128)} %param.28) | copy-start | bytes 6148
  47.1 8.8 %copy-start.5 = (bf16[512,512]{1,0:T(8,128)(2,1)S(1)}, bf16[512,512]{1,0:T(8,128)(2,1)}, u32[]{:S(2)}) copy-start(bf16[512,512]{1,0:T(8,128)(2,1)} %param.40) | copy-start | bytes 1572868
  47.2 20.8 %copy-start.6 = (bf16[512,512]{1,0:T(8,128)(2,1)S(1)}, bf16[512,512]{1,0:T(8,128)(2,1)}, u32[]{:S(2)}) copy-start(bf16[512,512]{1,0:T(8,128)(2,1)} %param.43) | copy-start | bytes 1572868
  50.6 5.5 %collective-permute-start.5 = (bf16[1,1,40,512]{3,2,1,0:T(8,128)(2,1)S(1)}, bf16[1,1,40,512]{3,2,1,0:T(8,128)(2,1)S(1)}, u32[]{:S(2)}, u32[]{:S(2)}) collective-permute-start(bf16[1,1,40,512]{3,2,1,0:T(8,128)(2,1)S(1)} %bitcast.56), channel_id=1, source_target_pairs={{16,0},{32,16},{48,32},{64,48},{80,64},{96,80},{112,96},{128,112},... | collective-permute-start | bytes 122888 | tf_op jit(solution)/shard_map/ppermute | solution.py:17
  54.0 8.1 %collective-permute-start.4 = (bf16[1,1,40,512]{3,2,1,0:T(8,128)(2,1)S(1)}, bf16[1,1,40,512]{3,2,1,0:T(8,128)(2,1)S(1)}, u32[]{:S(2)}, u32[]{:S(2)}) collective-permute-start(bf16[1,1,40,512]{3,2,1,0:T(8,128)(2,1)S(1)} %bitcast.57), channel_id=1, source_target_pairs={{0,16},{16,32},{32,48},{48,64},{64,80},{80,96},{96,112},{112,128},... | collective-permute-start | bytes 122888 | tf_op jit(solution)/shard_map/ppermute | solution.py:16
  62.1 6.8 %collective-permute-start.7 = (bf16[1,3,40,512]{3,2,1,0:T(8,128)(2,1)S(1)}, bf16[1,3,40,512]{3,2,1,0:T(8,128)(2,1)S(1)}, u32[]{:S(2)}, u32[]{:S(2)}) collective-permute-start(bf16[1,3,40,512]{3,2,1,0:T(8,128)(2,1)S(1)} %pad_maximum_fusion.6), channel_id=1, source_target_pairs={{1,0},{2,1},{3,2},{4,3},{5,4},{6,5},{7,6},{8,7},{9,8},{10,9},{11,1... | collective-permute-start | bytes 368648 | tf_op jit(solution)/shard_map/ppermute | solution.py:17
  67.9 2.4 %collective-permute-start.6 = (bf16[1,3,40,512]{3,2,1,0:T(8,128)(2,1)S(1)}, bf16[1,3,40,512]{3,2,1,0:T(8,128)(2,1)S(1)}, u32[]{:S(2)}, u32[]{:S(2)}) collective-permute-start(bf16[1,3,40,512]{3,2,1,0:T(8,128)(2,1)S(1)} %pad_maximum_fusion.6), channel_id=1, source_target_pairs={{0,1},{1,2},{2,3},{3,4},{4,5},{5,6},{6,7},{7,8},{8,9},{9,10},{10,1... | collective-permute-start | bytes 368648 | tf_op jit(solution)/shard_map/ppermute | solution.py:16
  178.4 2.0 %copy-start.3 = (bf16[512,512]{1,0:T(8,128)(2,1)S(1)}, bf16[512,512]{1,0:T(8,128)(2,1)}, u32[]{:S(2)}) copy-start(bf16[512,512]{1,0:T(8,128)(2,1)} %param.39) | copy-start | bytes 1572868
  180.4 0.7 copy-start.14
  180.4 0.7 copy-start.15
  180.4 1.0 copy-start.16
  181.5 1.0 copy-start.4
  182.5 1.4 copy-start.9
  182.5 1.5 copy-start.10
Sparse Core Ops, SparseCore 0:
  50.1 126.3 all-gather.2
where the time goes:
time: 193 us; the launch traced here: 192 us
  waiting for transfers between devices  114 us (59%)
  starting transfers between devices  34.5 us (18%)
  between operations  13.9 us (7%)
  matrix products  13.8 us (7%)
  local copies, waits for them, and re-layouts  11.6 us (6%)
  other arithmetic  4.26 us (2%)
    all_gather x1, waiting for transfers between devices, body(): coarse = lax.all_gather(encoded[0:1], ('lon', 'lat'), axis=0, tiled=True)  106 us
    ppermute x4, starting transfers between devices, padded(): after = lax.ppermute(first, axis, down)  24.6 us
    ppermute x4, starting transfers between devices, padded(): before = lax.ppermute(last, axis, up)  9.93 us
    ppermute x4, waiting for transfers between devices, padded(): before = lax.ppermute(last, axis, up)  7.32 us
    gather x1, local copies, waits for them, and re-layouts, body(): jnp.take(extended.reshape(-1, latent_width), grid_senders[0, 0], axis=0)  3.97 us
  transfers between devices with their start and end apart: 9, of which 4 were waited for; matrix products, arithmetic and copies ran while one was open for 4% of the time, Pallas kernels for 0%

commit v1 on v0

v1 whole, which is shorter than its diff:
```python
import functools

import jax
import jax.numpy as jnp
from jax import lax
from jax.experimental import pallas as pl
from jax.experimental.pallas import tpu as pltpu
from jax.sharding import PartitionSpec as P

MESH = pl.DeviceIdType.MESH
LATENT = 512
HALF = 256
GRID_LAT = 16
GRID_LON = 32
RIM = 3
SLOTS = 40
BLOCK = 48
GRID_EDGES = 1024
MESH_EDGES = 512
TILE = 256
OWN = GRID_LAT * GRID_LON
UP, DOWN, LEFT, RIGHT = 0, 96, 192, 240
CORNER = 288
HALO = 384
PACKED = 160
GEO = 96
BF16, F32, I32 = jnp.bfloat16, jnp.float32, jnp.int32


def dot(a, b):
    return jnp.dot(a, b, preferred_element_type=F32)


def silu(v):
    half = 0.5 * v
    return half + half * jnp.tanh(half)


def layer_norm(v):
    centre = jnp.mean(v, axis=-1, keepdims=True)
    shifted = v - centre
    spread = jnp.mean(shifted * shifted, axis=-1, keepdims=True)
    return shifted * lax.rsqrt(spread + 1e-5)


def lanes(rows, columns):
    return lax.broadcasted_iota(I32, (rows, columns), 1).astype(F32)


def one_hot(column, width):
    return jnp.where(lanes(column.shape[0], width) == column, 1.0, 0.0).astype(BF16)


def target_hot(columns):
    place = lanes(columns.shape[0], 128)
    target = columns[:, 5:6]
    hot = jnp.where((place == target) | (place == target + BLOCK), 1.0, 0.0)
    for f in range(4):
        hot = jnp.where(place == GEO + f, columns[:, f : f + 1], hot)
    return hot.astype(BF16)


def fill_target_table(table, nodes, w_target, w_geometry):
    term = dot(nodes, w_target)
    high = term.astype(BF16)
    table[...] = jnp.zeros_like(table)
    table[0:SLOTS, :] = high
    table[BLOCK : BLOCK + SLOTS, :] = (term - high.astype(F32)).astype(BF16)
    table[GEO : GEO + 4, :] = w_geometry


def incidence(targets, count):
    edges = targets.shape[1]
    slot = lax.broadcasted_iota(I32, (SLOTS, edges), 0)
    live = lax.broadcasted_iota(I32, (SLOTS, edges), 1) < count
    return jnp.where((slot == targets) & live, 1.0, 0.0).astype(BF16)


def transposed(rows):
    return jnp.transpose(jnp.concatenate(rows, axis=0), (1, 0))


def kernel(nx, ny, nlat, *refs):
    (
        grid_hbm, mesh_hbm, gs_hbm, gt_hbm, gg_hbm, ms_hbm, mt_hbm, mg_hbm, ec_hbm,
        es_hbm, et_hbm, eg_hbm, eo_hbm, ei_hbm, ein_hbm, ef_hbm,
        ps_hbm, pt_hbm, pg_hbm, po_hbm, pi_hbm, pin_hbm, pf_hbm,
        out_ref,
        x_v, nodes_v, gs_v, gt_v, gg_v, ms_v, mt_v, mg_v, ec_v,
        es_v, et_v, eg_v, eo_v, ei_v, ein_v, ef_v,
        ps_v, pt_v, pg_v, po_v, pi_v, pin_v, pf_v,
        own_t, packed, halo_t, tg_t, columns_v, halo_hot, base, inc, inflow,
        near_t, near_mine, mtg_t, mcolumns_v, near_hot, far_hot0, far_hot1, mbase, minc, minflow,
        row_mine, rows_in, far_t,
        in_sem, halo_ss, halo_rs, near_ss, near_rs, s1_ss, s1_rs, s2_ss, s2_rs, s3_ss, s3_rs, s4_ss, s4_rs,
    ) = refs
    nlon = nx * ny
    lon, lat = lax.axis_index("lon"), lax.axis_index("lat")
    core = lax.rem(lat, 2)
    x, y = lon // ny, lax.rem(lon, ny)
    first = jnp.where(core == 0, x, y)
    second = jnp.where(core == 0, y, x)
    first_step = jnp.where(core == 0, ny, 1)
    second_step = jnp.where(core == 0, 1, ny)

    sources = [
        (grid_hbm, x_v), (es_hbm, es_v),
        (mesh_hbm.at[0, 0], nodes_v), (gs_hbm.at[0], gs_v), (gt_hbm.at[0], gt_v), (gg_hbm.at[0, 0], gg_v),
        (ec_hbm, ec_v), (et_hbm, et_v), (eg_hbm, eg_v), (eo_hbm, eo_v), (ei_hbm, ei_v), (ein_hbm, ein_v),
        (ef_hbm, ef_v), (ps_hbm, ps_v), (ms_hbm.at[0], ms_v), (mt_hbm.at[0], mt_v), (mg_hbm.at[0, 0], mg_v),
        (pt_hbm, pt_v), (pg_hbm, pg_v), (po_hbm, po_v), (pi_hbm, pi_v), (pin_hbm, pin_v), (pf_hbm, pf_v),
    ]
    loads = [pltpu.make_async_copy(src, dst, in_sem.at[k]) for k, (src, dst) in enumerate(sources)]
    for load in loads:
        load.start()

    def turn(v, step, n):
        return lax.rem(v + step + n, n)

    around = [(0, 1), (0, -1), (1, 0), (-1, 0), (1, 1), (1, -1), (-1, 1), (-1, -1)]

    def neighbour(step):
        return (turn(lon, step[1], nlon), turn(lat, step[0], nlat))

    def first_peer(k):
        return (lax.rem(first + k, nx) * first_step + second * second_step, lat)

    def second_peer(k):
        return (first * first_step + lax.rem(second + k, nx) * second_step, lat)

    barrier = pltpu.get_barrier_semaphore()

    def greet(device):
        pl.semaphore_signal(barrier, inc=1, device_id=device, device_id_type=MESH)

    for step in around:
        if step[1] != 0:
            greet(neighbour(step))

    def greet_line(k, carry):
        greet((lon, lax.rem(lat + k, nlat)))
        return carry

    def greet_plane(k, carry):
        greet(first_peer(k))
        greet(second_peer(k))
        return carry

    lax.fori_loop(1, nlat, greet_line, 0)
    lax.fori_loop(1, nx, greet_plane, 0)

    loads[0].wait()
    loads[1].wait()

    def project_own(i, carry):
        rows = x_v[pl.ds(i * (TILE // GRID_LON), TILE // GRID_LON)].reshape(TILE, LATENT)
        own_t[pl.ds(pl.multiple_of(i * TILE, TILE), TILE), :] = dot(rows, es_v[...]).astype(BF16)
        return carry

    lax.fori_loop(0, OWN // TILE, project_own, 0)
    place = lax.broadcasted_iota(I32, (PACKED, 128), 0)
    side = jnp.where(place < 48, place, place - 48)
    third = (side * 43) >> 7
    edge_row = third * GRID_LON + (side - 3 * third) + jnp.where(place < 48, GRID_LON - RIM, 0)
    corner = (place - 96) & 15
    which = (place - 96) >> 4
    third = (corner * 43) >> 7
    corner_row = (third + jnp.where(which < 2, GRID_LAT - RIM, 0)) * GRID_LON + (corner - 3 * third)
    corner_row = corner_row + jnp.where((which & 1) == 0, GRID_LON - RIM, 0)
    corner_row = jnp.where(corner < 9, corner_row, -1)
    wanted = jnp.where(place < 96, edge_row, corner_row)
    wanted = jnp.concatenate([wanted] * (OWN // 128), axis=1)
    pick = jnp.where(lax.broadcasted_iota(I32, (PACKED, OWN), 1) == wanted, 1.0, 0.0).astype(BF16)
    packed[...] = dot(pick, own_t[...]).astype(BF16)

    pl.semaphore_wait(barrier, (nlat - 1) + 2 * (nx - 1) + 6)

    halo_moves = [
        (packed.at[pl.ds(0, 48)], LEFT, 48, (0, 1)),
        (packed.at[pl.ds(48, 48)], RIGHT, 48, (0, -1)),
        (own_t.at[pl.ds(OWN - 96, 96)], UP, 96, (1, 0)),
        (own_t.at[pl.ds(0, 96)], DOWN, 96, (-1, 0)),
        (packed.at[pl.ds(96, 16)], CORNER, 16, (1, 1)),
        (packed.at[pl.ds(112, 16)], CORNER + 16, 16, (1, -1)),
        (packed.at[pl.ds(128, 16)], CORNER + 32, 16, (-1, 1)),
        (packed.at[pl.ds(144, 16)], CORNER + 48, 16, (-1, -1)),
    ]
    halo_copies = [
        pltpu.make_async_remote_copy(
            src_ref=src, dst_ref=halo_t.at[pl.ds(at, rows)], send_sem=halo_ss.at[k], recv_sem=halo_rs.at[k],
            device_id=neighbour(step), device_id_type=MESH,
        )
        for k, (src, at, rows, step) in enumerate(halo_moves)
    ]
    for copy in halo_copies:
        copy.start()

    for load in loads[2:13]:
        load.wait()
    halo_t[pl.ds(352, 32), :] = jnp.zeros((32, LATENT), BF16)
    nodes = nodes_v[...]
    fill_target_table(tg_t, nodes, et_v[...], eg_v[...])
    s = gs_v[...]
    r = (s * 1725) >> 16
    c = s - r * (GRID_LON + 2 * RIM)
    above, below = r < RIM, r >= GRID_LAT + RIM
    before, after = c < RIM, c >= GRID_LON + RIM
    row_in = jnp.where(above, r, jnp.where(below, r - GRID_LAT - RIM, r - RIM))
    col_in = jnp.where(before, c, jnp.where(after, c - GRID_LON - RIM, c - RIM))
    beside, over = before | after, above | below
    wide = row_in * GRID_LON + col_in
    thin = row_in * RIM + col_in
    own_at = jnp.where(beside | over, -1, wide)
    over_at = wide + jnp.where(above, UP, DOWN)
    beside_at = thin + jnp.where(before, LEFT, RIGHT)
    corner_at = thin + CORNER + jnp.where(above, 0, 32) + jnp.where(before, 0, 16)
    halo_at = jnp.where(over, jnp.where(beside, corner_at, over_at), jnp.where(beside, beside_at, -1))
    targets = gt_v[...]
    columns_v[...] = transposed([
        gg_v[...].astype(F32), own_at.astype(F32), targets.astype(F32), halo_at.astype(F32),
        jnp.zeros((1, GRID_EDGES), F32),
    ])
    inc[...] = incidence(targets, ec_v[0])
    inflow[...] = jnp.zeros_like(inflow)

    def grid_base(i, carry):
        edges = pl.ds(pl.multiple_of(i * TILE, TILE), TILE)
        columns = columns_v[edges, :]
        total = dot(one_hot(columns[:, 4:5], OWN), own_t[...])
        base[edges, :] = total + dot(target_hot(columns), tg_t[...])
        halo_hot[edges, :] = one_hot(columns[:, 6:7], HALO)
        return carry

    lax.fori_loop(0, GRID_EDGES // TILE, grid_base, 0)
    self_term = dot(nodes, ei_v[...])

    for copy in halo_copies:
        copy.wait_recv()

    def grid_edges(i, carry):
        edges = pl.ds(pl.multiple_of(i * TILE, TILE), TILE)
        hidden = silu(base[edges, :] + dot(halo_hot[edges, :], halo_t[...])).astype(BF16)
        message = layer_norm(dot(hidden, eo_v[...])).astype(BF16)
        inflow[...] += dot(inc[:, edges], message)
        return carry

    lax.fori_loop(0, GRID_EDGES // TILE, grid_edges, 0)
    hidden = silu(self_term + dot(inflow[...].astype(BF16), ein_v[...])).astype(BF16)
    encoded = (nodes.astype(F32) + layer_norm(dot(hidden, ef_v[...]))).astype(BF16)
    loads[13].wait()
    term = dot(encoded, ps_v[...]).astype(BF16)

    row_mine[...] = term.astype(F32)[0:1, :]

    def line_copy(k):
        return pltpu.make_async_remote_copy(
            src_ref=row_mine, dst_ref=rows_in.at[lat], send_sem=s1_ss.at[k], recv_sem=s1_rs.at[lat],
            device_id=(lon, lax.rem(lat + k, nlat)), device_id_type=MESH,
        )

    def line_arrival(k):
        source = lax.rem(lat + k, nlat)
        return pltpu.make_async_remote_copy(
            src_ref=row_mine, dst_ref=rows_in.at[source], send_sem=s1_ss.at[k], recv_sem=s1_rs.at[source],
            device_id=(lon, source), device_id_type=MESH,
        )

    def start_line(k, carry):
        line_copy(k).start()
        return carry

    lax.fori_loop(1, nlat, start_line, 0)

    near_mine[0:SLOTS, :] = term
    near_mine[SLOTS:BLOCK, :] = jnp.zeros((BLOCK - SLOTS, LATENT), BF16)
    near_copies = []
    for k, step in enumerate(around):
        at = ((1 - step[0]) * 3 + (1 - step[1])) * BLOCK
        copy = pltpu.make_async_remote_copy(
            src_ref=near_mine, dst_ref=near_t.at[pl.ds(at, BLOCK)], send_sem=near_ss.at[k], recv_sem=near_rs.at[k],
            device_id=neighbour(step), device_id_type=MESH,
        )
        copy.start()
        near_copies.append(copy)
    near_t[pl.ds(4 * BLOCK, BLOCK), :] = near_mine[...]
    near_t[pl.ds(9 * BLOCK, 512 - 9 * BLOCK), :] = jnp.zeros((512 - 9 * BLOCK, LATENT), BF16)

    for load in loads[14:23]:
        load.wait()
    fill_target_table(mtg_t, encoded, pt_v[...], pg_v[...])
    s = ms_v[...]
    near = s < 9 * SLOTS
    sector = (s * 1639) >> 16
    near_at = jnp.where(near, sector * BLOCK + (s - sector * SLOTS), -1)
    t = s - 9 * SLOTS
    plane, line = t // nlat, lax.rem(t, nlat)
    far_x, far_y = plane // ny, lax.rem(plane, ny)
    far_at0 = jnp.where(near, -1, (far_y * nx + far_x) * nlat + line)
    far_at1 = jnp.where(near, -1, t)
    targets = mt_v[...]
    mcolumns_v[...] = transposed([
        mg_v[...].astype(F32), near_at.astype(F32), targets.astype(F32), far_at0.astype(F32), far_at1.astype(F32),
    ])
    minc[...] = incidence(targets, ec_v[1])
    minflow[...] = jnp.zeros_like(minflow)

    def mesh_hot(i, carry):
        edges = pl.ds(pl.multiple_of(i * TILE, TILE), TILE)
        columns = mcolumns_v[edges, :]
        near_hot[edges, :] = one_hot(columns[:, 4:5], 512)
        mbase[edges, :] = dot(target_hot(columns), mtg_t[...])
        far_hot0[edges, :] = one_hot(columns[:, 6:7], nlon * nlat)
        far_hot1[edges, :] = one_hot(columns[:, 7:8], nlon * nlat)
        return carry

    lax.fori_loop(0, MESH_EDGES // TILE, mesh_hot, 0)
    mself_term = dot(encoded, pi_v[...])

    def wait_line(k, carry):
        line_arrival(k).wait_recv()
        return carry

    lax.fori_loop(1, nlat, wait_line, 0)
    line_row = lax.broadcasted_iota(I32, (nlat, LATENT), 0)
    block = jnp.where(line_row == lat, row_mine[...], 0.0)
    for k in range(nlat):
        block = jnp.where((line_row == k) & (lat != k), rows_in[k], block)
    half = jnp.where(core == 0, block[:, :HALF], block[:, HALF:])
    far_t[core, second, first] = half.astype(BF16)

    def stage2(k, source):
        at = far_t.at[core, second, source]
        return pltpu.make_async_remote_copy(
            src_ref=at, dst_ref=at, send_sem=s2_ss.at[k], recv_sem=s2_rs.at[source],
            device_id=first_peer(k), device_id_type=MESH,
        )

    def stage3(k, source):
        at = far_t.at[core, source]
        return pltpu.make_async_remote_copy(
            src_ref=at, dst_ref=at, send_sem=s3_ss.at[k], recv_sem=s3_rs.at[source],
            device_id=second_peer(k), device_id_type=MESH,
        )

    def stage4(half_of, source):
        at = far_t.at[half_of, source]
        return pltpu.make_async_remote_copy(
            src_ref=at, dst_ref=at, send_sem=s4_ss.at[source], recv_sem=s4_rs.at[source],
            device_id=(lon, lat + 1 - 2 * core), device_id_type=MESH,
        )

    for k in range(1, nx):
        stage2(k, first).start()
    for k in range(1, nx):
        stage2(k, lax.rem(first + k, nx)).wait_recv()

    for k in range(1, nx):
        stage3(k, second).start()
    stage4(core, second).start()

    for copy in near_copies:
        copy.wait_recv()

    def near_base(i, carry):
        edges = pl.ds(pl.multiple_of(i * TILE, TILE), TILE)
        mbase[edges, :] += dot(near_hot[edges, :], near_t[...])
        return carry

    lax.fori_loop(0, MESH_EDGES // TILE, near_base, 0)

    order = sorted(range(1, nx), key=lambda k: min(k, nx - k))
    for k in order:
        source = lax.rem(second + k, nx)
        stage3(k, source).wait_recv()
        stage4(core, source).start()
    for k in range(nx):
        stage4(1 - core, k).wait_recv()

    table0 = far_t[0].reshape(nlon * nlat, HALF)
    table1 = far_t[1].reshape(nlon * nlat, HALF)

    def mesh_edges(i, carry):
        edges = pl.ds(pl.multiple_of(i * TILE, TILE), TILE)
        far = jnp.concatenate([dot(far_hot0[edges, :], table0), dot(far_hot1[edges, :], table1)], axis=1)
        hidden = silu(mbase[edges, :] + far).astype(BF16)
        message = layer_norm(dot(hidden, po_v[...])).astype(BF16)
        minflow[...] += dot(minc[:, edges], message)
        return carry

    lax.fori_loop(0, MESH_EDGES // TILE, mesh_edges, 0)
    hidden = silu(mself_term + dot(minflow[...].astype(BF16), pin_v[...])).astype(BF16)
    update = layer_norm(dot(hidden, pf_v[...]))
    out_ref[0, 0] = (encoded.astype(F32) + update).astype(BF16)

    for copy in halo_copies:
        copy.wait_send()
    for copy in near_copies:
        copy.wait_send()

    def end_line(k, carry):
        line_copy(k).wait_send()
        return carry

    lax.fori_loop(1, nlat, end_line, 0)
    for k in range(1, nx):
        stage2(k, first).wait_send()
        stage3(k, second).wait_send()
    for k in range(nx):
        stage4(core, k).wait_send()


def body(nx, ny, nlat, *args):
    weight = pltpu.VMEM((LATENT, LATENT), BF16)
    narrow = pltpu.VMEM((4, LATENT), BF16)
    far = nx * ny * nlat
    dma = pltpu.SemaphoreType.DMA
    scratch = [
        pltpu.VMEM((GRID_LAT, GRID_LON, LATENT), BF16), pltpu.VMEM((SLOTS, LATENT), BF16),
        pltpu.VMEM((1, GRID_EDGES), I32), pltpu.VMEM((1, GRID_EDGES), I32), pltpu.VMEM((4, GRID_EDGES), BF16),
        pltpu.VMEM((1, MESH_EDGES), I32), pltpu.VMEM((1, MESH_EDGES), I32), pltpu.VMEM((4, MESH_EDGES), BF16),
        pltpu.VMEM((2, 1, 1), I32),
        weight, weight, narrow, weight, weight, weight, weight,
        weight, weight, narrow, weight, weight, weight, weight,
        pltpu.VMEM((OWN, LATENT), BF16), pltpu.VMEM((PACKED, LATENT), BF16), pltpu.VMEM((HALO, LATENT), BF16),
        pltpu.VMEM((128, LATENT), BF16), pltpu.VMEM((GRID_EDGES, 8), F32), pltpu.VMEM((GRID_EDGES, HALO), BF16),
        pltpu.VMEM((GRID_EDGES, LATENT), F32), pltpu.VMEM((SLOTS, GRID_EDGES), BF16), pltpu.VMEM((SLOTS, LATENT), F32),
        pltpu.VMEM((512, LATENT), BF16), pltpu.VMEM((BLOCK, LATENT), BF16),
        pltpu.VMEM((128, LATENT), BF16), pltpu.VMEM((MESH_EDGES, 8), F32), pltpu.VMEM((MESH_EDGES, 512), BF16),
        pltpu.VMEM((MESH_EDGES, far), BF16), pltpu.VMEM((MESH_EDGES, far), BF16),
        pltpu.VMEM((MESH_EDGES, LATENT), F32), pltpu.VMEM((SLOTS, MESH_EDGES), BF16), pltpu.VMEM((SLOTS, LATENT), F32),
        pltpu.VMEM((1, LATENT), F32), pltpu.VMEM((nlat, 1, LATENT), F32), pltpu.VMEM((2, nx, nx, nlat, HALF), BF16),
        dma((23,)), dma((8,)), dma((8,)), dma((8,)), dma((8,)), dma((nlat,)), dma((nlat,)),
        dma((nx,)), dma((nx,)), dma((nx,)), dma((nx,)), dma((nx,)), dma((nx,)),
    ]
    return pl.pallas_call(
        functools.partial(kernel, nx, ny, nlat),
        out_shape=jax.ShapeDtypeStruct((1, 1, SLOTS, LATENT), BF16),
        in_specs=[pl.BlockSpec(memory_space=pl.ANY)] * 23,
        out_specs=pl.BlockSpec(memory_space=pltpu.VMEM),
        scratch_shapes=scratch,
        compiler_params=pltpu.CompilerParams(collective_id=0, has_side_effects=True, vmem_limit_bytes=60 * 2**20),
        cost_estimate=pl.CostEstimate(flops=3 * 10**9, bytes_accessed=6 * 10**6, transcendentals=10**6),
    )(*args)


def solution(mesh):
    nlon, nlat = mesh.shape["lon"], mesh.shape["lat"]
    nx = round(nlon**0.5)
    return jax.shard_map(
        functools.partial(body, nx, nlon // nx, nlat),
        mesh=mesh,
        in_specs=(
            P("lat", "lon", None),
            P("lat", "lon", None, None),
            P("lat", "lon", None),
            P("lat", "lon", None),
            P("lat", "lon", None, None),
            P("lat", "lon", None),
            P("lat", "lon", None),
            P("lat", "lon", None, None),
            P(None, "lat", "lon"),
        )
        + (P(),) * 14,
        out_specs=P("lat", "lon", None, None),
        check_vma=False,
    )
```

time: 193 us -> 60.3 us (0.31)
  waiting for transfers between devices: 114 us -> 0 us
  Pallas kernels: 0 us -> 57.4 us
  starting transfers between devices: 34.5 us -> 0 us
  between operations: 13.9 us -> 0.01 us
  matrix products: 13.8 us -> 0 us
  local copies, waits for them, and re-layouts: 11.6 us -> 2.69 us
  other arithmetic: 4.26 us -> 0 us
    all_gather x1 -> x0, waiting for transfers between devices: 106 us -> none  [body(): coarse = lax.all_gather(encoded[0:1], ('lon', 'lat'), axis=0, tiled=True)]
    pallas_call x0 -> x1, Pallas kernels: none -> 57.4 us  [body(): pl.pallas_call(functools.partial(kernel, nx, ny, nlat), out_shape=jax.Sha...]
    ppermute x8 -> x0, starting transfers between devices: 34.5 us -> none  [the longest x4 24.6 us: padded(): after = lax.ppermute(first, axis, down)]
    dot_general x16 -> x0, matrix products: 13.8 us -> none  [the longest x2 2.89 us: edge_update(): lax.dot_general(geometry, w_geometry, (((0,), (0,)), ((), ())), preferred...]
    ppermute x8 -> x0, waiting for transfers between devices: 8.12 us -> none  [the longest x4 7.32 us: padded(): before = lax.ppermute(last, axis, up)]
    gather x2 -> x0, local copies, waits for them, and re-layouts: 5.94 us -> none  [the longest x1 3.97 us: body(): jnp.take(extended.reshape(-1, latent_width), grid_senders[0, 0], axis=0)]
  transfers between devices with their start and end apart: 9 -> 0, of which waited for: 4 -> 0; matrix products, arithmetic and copies ran while one was open for 4% -> 0% of each run, Pallas kernels for 0% -> 0%
where the time goes in v1:
time: 60.3 us; the launch traced here: 60.1 us
  Pallas kernels  57.4 us (95%)
  local copies, waits for them, and re-layouts  2.69 us (4%)
    pallas_call x1, Pallas kernels, body(): pl.pallas_call(functools.partial(kernel, nx, ny, nlat), out_shape=jax.Sha...  57.4 us
    unnamed x2, local copies, waits for them, and re-layouts  2.69 us

profile of v1, /device:TPU:1, one launch (start us, length us, event | category | flops | bytes accessed | tf_op | source)
XLA Modules:
  0.0 60.1 jit_solution(9059338112510665628)
XLA Ops:
  0.0 1.3 %copy.24.refs_8_ = s32[2,1,1]{2,1,0:T(1,128)} copy(s32[2,1,1]{0,2,1:T(1,128)} %param.31) | data formatting | bytes 16 | tf_op args[8]
  1.3 57.4 %shard_map.217 = bf16[1,1,40,512]{3,2,1,0:T(8,128)(2,1)} custom-call(bf16[16,32,512]{2,1,0:T(8,128)(2,1)} %refs_0_.1, bf16[1,1,40,512]{3,2,1,0:T(8,128)(2,1)} %refs_1_.1, s32[1,1,1024]{2,1,0:T(1,128)} %refs_2_.1, s32[1,1,1024]{2,1,0:T(1,128)} %refs_3_.1, bf16[1,1,4,1024]{3,2,1,0:T(4,128)(2,1)} %refs_4_.1, s32[1,1,512]{2,1,0:T(1,128)} %refs_5_.1, ...), custom_call_target="tpu_custom_call" | custom-call | flops 3000000000 | bytes 6000000 | tf_op jit(solution)/shard_map/pallas_call | solution.py:435
  58.7 1.4 %copy.26 = bf16[1,1,40,512]{3,2,1,0:T(8,128)(2,1)} copy(bf16[1,1,40,512]{3,2,1,0:T(8,128)(2,1)} %shard_map.217) | data formatting | bytes 81920

commit v2 on v1

--- a/solution.py
+++ b/solution.py
@@ -90,11 +90,11 @@
         es_v, et_v, eg_v, eo_v, ei_v, ein_v, ef_v,
         ps_v, pt_v, pg_v, po_v, pi_v, pin_v, pf_v,
         own_t, packed, halo_t, tg_t, columns_v, halo_hot, base, inc, inflow,
-        near_t, near_mine, mtg_t, mcolumns_v, near_hot, far_hot0, far_hot1, mbase, minc, minflow,
+        near_t, mtg_t, mcolumns_v, near_hot, far_hot, mbase, minc, minflow,
         row_mine, rows_in, far_t,
-        in_sem, halo_ss, halo_rs, near_ss, near_rs, s1_ss, s1_rs, s2_ss, s2_rs, s3_ss, s3_rs, s4_ss, s4_rs,
+        in_sem, late_sem, halo_ss, halo_rs, near_ss, near_rs, s1_ss, s1_rs, s2_ss, s2_rs, s3_ss, s3_rs, s4_ss, s4_rs,
     ) = refs
-    nlon = nx * ny
+    nlon, half_line = nx * ny, nlat // 2
     lon, lat = lax.axis_index("lon"), lax.axis_index("lat")
     core = lax.rem(lat, 2)
     x, y = lon // ny, lax.rem(lon, ny)
@@ -102,6 +102,10 @@
     second = jnp.where(core == 0, y, x)
     first_step = jnp.where(core == 0, ny, 1)
     second_step = jnp.where(core == 0, 1, ny)
+    group = lat // half_line
+    other = 1 - group
+    place_in_line = lax.rem(lat, half_line)
+    has_above, has_below = lat > 0, lat < nlat - 1
 
     sources = [
         (grid_hbm, x_v), (es_hbm, es_v),
@@ -111,16 +115,25 @@
         (pt_hbm, pt_v), (pg_hbm, pg_v), (po_hbm, po_v), (pi_hbm, pi_v), (pin_hbm, pin_v), (pf_hbm, pf_v),
     ]
     loads = [pltpu.make_async_copy(src, dst, in_sem.at[k]) for k, (src, dst) in enumerate(sources)]
-    for load in loads:
-        load.start()
-
-    def turn(v, step, n):
-        return lax.rem(v + step + n, n)
+    loads[0].start()
+    loads[1].start()
 
     around = [(0, 1), (0, -1), (1, 0), (-1, 0), (1, 1), (1, -1), (-1, 1), (-1, -1)]
 
     def neighbour(step):
-        return (turn(lon, step[1], nlon), turn(lat, step[0], nlat))
+        return (lax.rem(lon + step[1] + nlon, nlon), lat + step[0])
+
+    def receives(step):
+        return {0: None, 1: has_above, -1: has_below}[step[0]]
+
+    def sends(step):
+        return {0: None, 1: has_below, -1: has_above}[step[0]]
+
+    def guarded(condition, act):
+        if condition is None:
+            act()
+        else:
+            pl.when(condition)(act)
 
     def first_peer(k):
         return (lax.rem(first + k, nx) * first_step + second * second_step, lat)
@@ -128,6 +141,9 @@
     def second_peer(k):
         return (first * first_step + lax.rem(second + k, nx) * second_step, lat)
 
+    def group_mate(k):
+        return group * half_line + lax.rem(place_in_line + k, half_line)
+
     barrier = pltpu.get_barrier_semaphore()
 
     def greet(device):
@@ -135,10 +151,18 @@
 
     for step in around:
         if step[1] != 0:
-            greet(neighbour(step))
-
-    def greet_line(k, carry):
-        greet((lon, lax.rem(lat + k, nlat)))
+            guarded(sends(step), functools.partial(greet, neighbour(step)))
+
+    @pl.when(lat == half_line)
+    def _():
+        greet((lon, half_line - 1))
+
+    def greet_mate(k, carry):
+        greet((lon, group_mate(k)))
+        return carry
+
+    def greet_upper(k, carry):
+        greet((lon, half_line + k))
         return carry
 
     def greet_plane(k, carry):
@@ -146,11 +170,20 @@
         greet(second_peer(k))
         return carry
 
-    lax.fori_loop(1, nlat, greet_line, 0)
+    lax.fori_loop(1, half_line, greet_mate, 0)
     lax.fori_loop(1, nx, greet_plane, 0)
+
+    @pl.when(group == 0)
+    def _():
+        lax.fori_loop(0, half_line, greet_upper, 0)
+
+    greetings = 2 + 2 * jnp.where(has_above, 1, 0) + 2 * jnp.where(has_below, 1, 0) + 2 * (nx - 1) + half_line - 1
+    greetings = greetings + jnp.where(group == 1, half_line, jnp.where(lat == half_line - 1, 1, 0))
 
     loads[0].wait()
     loads[1].wait()
+    for load in loads[2:14]:
+        load.start()
 
     def project_own(i, carry):
         rows = x_v[pl.ds(i * (TILE // GRID_LON), TILE // GRID_LON)].reshape(TILE, LATENT)
@@ -173,7 +206,7 @@
     pick = jnp.where(lax.broadcasted_iota(I32, (PACKED, OWN), 1) == wanted, 1.0, 0.0).astype(BF16)
     packed[...] = dot(pick, own_t[...]).astype(BF16)
 
-    pl.semaphore_wait(barrier, (nlat - 1) + 2 * (nx - 1) + 6)
+    pl.semaphore_wait(barrier, greetings)
 
     halo_moves = [
         (packed.at[pl.ds(0, 48)], LEFT, 48, (0, 1)),
@@ -192,8 +225,34 @@
         )
         for k, (src, at, rows, step) in enumerate(halo_moves)
     ]
-    for copy in halo_copies:
-        copy.start()
+    for copy, (*_, step) in zip(halo_copies, halo_moves):
+        guarded(sends(step), copy.start)
+
+    @pl.when(group == 1)
+    def _():
+        def report(k, carry):
+            pl.semaphore_signal(late_sem, inc=1, device_id=(lon, k), device_id_type=MESH)
+            return carry
+
+        lax.fori_loop(0, half_line, report, 0)
+
+    for load in loads[14:]:
+        load.start()
+
+    def no_sector(at, rows):
+        halo_t[pl.ds(at, rows), :] = jnp.zeros((rows, LATENT), BF16)
+
+    @pl.when(lat == 0)
+    def _():
+        no_sector(UP, 96)
+        no_sector(CORNER, 32)
+        near_t[pl.ds(0, 3 * BLOCK), :] = jnp.zeros((3 * BLOCK, LATENT), BF16)
+
+    @pl.when(lat == nlat - 1)
+    def _():
+        no_sector(DOWN, 96)
+        no_sector(CORNER + 32, 32)
+        near_t[pl.ds(6 * BLOCK, 3 * BLOCK), :] = jnp.zeros((3 * BLOCK, LATENT), BF16)
 
     for load in loads[2:13]:
         load.wait()
@@ -220,7 +279,7 @@
         gg_v[...].astype(F32), own_at.astype(F32), targets.astype(F32), halo_at.astype(F32),
         jnp.zeros((1, GRID_EDGES), F32),
     ])
-    inc[...] = incidence(targets, ec_v[0])
+    inc[...] = incidence(targets, ec_v[0, :, 0:1])
     inflow[...] = jnp.zeros_like(inflow)
 
     def grid_base(i, carry):
@@ -234,8 +293,8 @@
     lax.fori_loop(0, GRID_EDGES // TILE, grid_base, 0)
     self_term = dot(nodes, ei_v[...])
 
-    for copy in halo_copies:
-        copy.wait_recv()
+    for copy, (*_, step) in zip(halo_copies, halo_moves):
+        guarded(receives(step), copy.wait_recv)
 
     def grid_edges(i, carry):
         edges = pl.ds(pl.multiple_of(i * TILE, TILE), TILE)
@@ -251,57 +310,67 @@
     term = dot(encoded, ps_v[...]).astype(BF16)
 
     row_mine[...] = term.astype(F32)[0:1, :]
-
-    def line_copy(k):
+    rows_in[lat] = term.astype(F32)[0:1, :]
+
+    def line_copy(target):
         return pltpu.make_async_remote_copy(
-            src_ref=row_mine, dst_ref=rows_in.at[lat], send_sem=s1_ss.at[k], recv_sem=s1_rs.at[lat],
-            device_id=(lon, lax.rem(lat + k, nlat)), device_id_type=MESH,
-        )
-
-    def line_arrival(k):
-        source = lax.rem(lat + k, nlat)
+            src_ref=row_mine, dst_ref=rows_in.at[lat], send_sem=s1_ss.at[target], recv_sem=s1_rs.at[lat],
+            device_id=(lon, target), device_id_type=MESH,
+        )
+
+    def line_arrival(source):
         return pltpu.make_async_remote_copy(
-            src_ref=row_mine, dst_ref=rows_in.at[source], send_sem=s1_ss.at[k], recv_sem=s1_rs.at[source],
+            src_ref=row_mine, dst_ref=rows_in.at[source], send_sem=s1_ss.at[source], recv_sem=s1_rs.at[source],
             device_id=(lon, source), device_id_type=MESH,
         )
 
-    def start_line(k, carry):
-        line_copy(k).start()
-        return carry
-
-    lax.fori_loop(1, nlat, start_line, 0)
-
-    near_mine[0:SLOTS, :] = term
-    near_mine[SLOTS:BLOCK, :] = jnp.zeros((BLOCK - SLOTS, LATENT), BF16)
-    near_copies = []
-    for k, step in enumerate(around):
-        at = ((1 - step[0]) * 3 + (1 - step[1])) * BLOCK
-        copy = pltpu.make_async_remote_copy(
-            src_ref=near_mine, dst_ref=near_t.at[pl.ds(at, BLOCK)], send_sem=near_ss.at[k], recv_sem=near_rs.at[k],
-            device_id=neighbour(step), device_id_type=MESH,
-        )
-        copy.start()
-        near_copies.append(copy)
-    near_t[pl.ds(4 * BLOCK, BLOCK), :] = near_mine[...]
+    def send_mate(k, carry):
+        line_copy(group_mate(k)).start()
+        return carry
+
+    def send_other(k, carry):
+        line_copy(other * half_line + k).start()
+        return carry
+
+    @pl.when(group == 1)
+    def _():
+        lax.fori_loop(0, half_line, send_other, 0)
+
+    lax.fori_loop(1, half_line, send_mate, 0)
+
+    near_t[pl.ds(4 * BLOCK, SLOTS), :] = term
+    near_t[pl.ds(4 * BLOCK + SLOTS, BLOCK - SLOTS), :] = jnp.zeros((BLOCK - SLOTS, LATENT), BF16)
     near_t[pl.ds(9 * BLOCK, 512 - 9 * BLOCK), :] = jnp.zeros((512 - 9 * BLOCK, LATENT), BF16)
+    near_moves = [(4, 3, 1, (0, 1)), (4, 5, 1, (0, -1)), (3, 0, 3, (1, 0)), (3, 6, 3, (-1, 0))]
+    near_copies = [
+        pltpu.make_async_remote_copy(
+            src_ref=near_t.at[pl.ds(source * BLOCK, blocks * BLOCK)], dst_ref=near_t.at[pl.ds(at * BLOCK, blocks * BLOCK)],
+            send_sem=near_ss.at[k], recv_sem=near_rs.at[k], device_id=neighbour(step), device_id_type=MESH,
+        )
+        for k, (source, at, blocks, step) in enumerate(near_moves)
+    ]
+    near_copies[0].start()
+    near_copies[1].start()
 
     for load in loads[14:23]:
         load.wait()
     fill_target_table(mtg_t, encoded, pt_v[...], pg_v[...])
     s = ms_v[...]
+    sectors = nlon * half_line
     near = s < 9 * SLOTS
     sector = (s * 1639) >> 16
     near_at = jnp.where(near, sector * BLOCK + (s - sector * SLOTS), -1)
     t = s - 9 * SLOTS
     plane, line = t // nlat, lax.rem(t, nlat)
     far_x, far_y = plane // ny, lax.rem(plane, ny)
-    far_at0 = jnp.where(near, -1, (far_y * nx + far_x) * nlat + line)
-    far_at1 = jnp.where(near, -1, t)
+    offset = (line // half_line) * sectors + lax.rem(line, half_line)
+    far_at0 = jnp.where(near, -1, (far_y * nx + far_x) * half_line + offset)
+    far_at1 = jnp.where(near, -1, plane * half_line + offset)
     targets = mt_v[...]
     mcolumns_v[...] = transposed([
         mg_v[...].astype(F32), near_at.astype(F32), targets.astype(F32), far_at0.astype(F32), far_at1.astype(F32),
     ])
-    minc[...] = incidence(targets, ec_v[1])
+    minc[...] = incidence(targets, ec_v[0, :, 1:2])
     minflow[...] = jnp.zeros_like(minflow)
 
     def mesh_hot(i, carry):
@@ -309,57 +378,94 @@
         columns = mcolumns_v[edges, :]
         near_hot[edges, :] = one_hot(columns[:, 4:5], 512)
         mbase[edges, :] = dot(target_hot(columns), mtg_t[...])
-        far_hot0[edges, :] = one_hot(columns[:, 6:7], nlon * nlat)
-        far_hot1[edges, :] = one_hot(columns[:, 7:8], nlon * nlat)
+        for g in range(2):
+            far_hot[0, g, edges, :] = one_hot(columns[:, 6:7] - g * sectors, sectors)
+            far_hot[1, g, edges, :] = one_hot(columns[:, 7:8] - g * sectors, sectors)
         return carry
 
     lax.fori_loop(0, MESH_EDGES // TILE, mesh_hot, 0)
     mself_term = dot(encoded, pi_v[...])
 
-    def wait_line(k, carry):
-        line_arrival(k).wait_recv()
-        return carry
-
-    lax.fori_loop(1, nlat, wait_line, 0)
-    line_row = lax.broadcasted_iota(I32, (nlat, LATENT), 0)
-    block = jnp.where(line_row == lat, row_mine[...], 0.0)
-    for k in range(nlat):
-        block = jnp.where((line_row == k) & (lat != k), rows_in[k], block)
-    half = jnp.where(core == 0, block[:, :HALF], block[:, HALF:])
-    far_t[core, second, first] = half.astype(BF16)
-
-    def stage2(k, source):
-        at = far_t.at[core, second, source]
+    near_copies[0].wait_recv()
+    near_copies[1].wait_recv()
+    for k in (2, 3):
+        guarded(sends(near_moves[k][3]), near_copies[k].start)
+
+    def place_rows(which):
+        row_at = lax.broadcasted_iota(I32, (half_line, LATENT), 0)
+        block = jnp.zeros((half_line, LATENT), F32)
+        for k in range(half_line):
+            block = jnp.where(row_at == k, rows_in[which * half_line + k], block)
+        half = jnp.where(core == 0, block[:, :HALF], block[:, HALF:])
+        far_t[which, core, second, first] = half.astype(BF16)
+
+    def stage2(turn, which, k, source):
+        at = far_t.at[which, core, second, source]
         return pltpu.make_async_remote_copy(
-            src_ref=at, dst_ref=at, send_sem=s2_ss.at[k], recv_sem=s2_rs.at[source],
+            src_ref=at, dst_ref=at, send_sem=s2_ss.at[turn, k], recv_sem=s2_rs.at[turn, source],
             device_id=first_peer(k), device_id_type=MESH,
         )
 
-    def stage3(k, source):
-        at = far_t.at[core, source]
+    def stage3(turn, which, k, source):
+        at = far_t.at[which, core, source]
         return pltpu.make_async_remote_copy(
-            src_ref=at, dst_ref=at, send_sem=s3_ss.at[k], recv_sem=s3_rs.at[source],
+            src_ref=at, dst_ref=at, send_sem=s3_ss.at[turn, k], recv_sem=s3_rs.at[turn, source],
             device_id=second_peer(k), device_id_type=MESH,
         )
 
-    def stage4(half_of, source):
-        at = far_t.at[half_of, source]
+    def stage4(turn, which, half_of, source):
+        at = far_t.at[which, half_of, source]
         return pltpu.make_async_remote_copy(
-            src_ref=at, dst_ref=at, send_sem=s4_ss.at[source], recv_sem=s4_rs.at[source],
+            src_ref=at, dst_ref=at, send_sem=s4_ss.at[turn, source], recv_sem=s4_rs.at[turn, source],
             device_id=(lon, lat + 1 - 2 * core), device_id_type=MESH,
         )
 
-    for k in range(1, nx):
-        stage2(k, first).start()
-    for k in range(1, nx):
-        stage2(k, lax.rem(first + k, nx)).wait_recv()
-
-    for k in range(1, nx):
-        stage3(k, second).start()
-    stage4(core, second).start()
-
-    for copy in near_copies:
-        copy.wait_recv()
+    order = sorted(range(1, nx), key=lambda k: min(k, nx - k))
+
+    def start2(turn, which):
+        for k in range(1, nx):
+            stage2(turn, which, k, first).start()
+
+    def start3(turn, which):
+        for k in range(1, nx):
+            stage2(turn, which, k, lax.rem(first + k, nx)).wait_recv()
+        for k in range(1, nx):
+            stage3(turn, which, k, second).start()
+        stage4(turn, which, core, second).start()
+
+    def hand_on(turn, which):
+        for k in order:
+            source = lax.rem(second + k, nx)
+            stage3(turn, which, k, source).wait_recv()
+            stage4(turn, which, core, source).start()
+
+    def wait4(turn, which):
+        for k in range(nx):
+            stage4(turn, which, 1 - core, k).wait_recv()
+
+    def far_part(which, edges):
+        parts = [dot(far_hot[h, which, edges, :], far_t[which, h].reshape(sectors, HALF)) for h in range(2)]
+        return jnp.concatenate(parts, axis=1)
+
+    def wait_mate(k, carry):
+        line_arrival(group_mate(k)).wait_recv()
+        return carry
+
+    def wait_other(k, carry):
+        line_arrival(other * half_line + k).wait_recv()
+        return carry
+
+    lax.fori_loop(1, half_line, wait_mate, 0)
+    place_rows(group)
+    start2(0, group)
+
+    @pl.when(group == 0)
+    def _():
+        pl.semaphore_wait(late_sem, half_line)
+        lax.fori_loop(0, half_line, send_other, 0)
+
+    for k in (2, 3):
+        guarded(receives(near_moves[k][3]), near_copies[k].wait_recv)
 
     def near_base(i, carry):
         edges = pl.ds(pl.multiple_of(i * TILE, TILE), TILE)
@@ -367,22 +473,26 @@
         return carry
 
     lax.fori_loop(0, MESH_EDGES // TILE, near_base, 0)
-
-    order = sorted(range(1, nx), key=lambda k: min(k, nx - k))
-    for k in order:
-        source = lax.rem(second + k, nx)
-        stage3(k, source).wait_recv()
-        stage4(core, source).start()
-    for k in range(nx):
-        stage4(1 - core, k).wait_recv()
-
-    table0 = far_t[0].reshape(nlon * nlat, HALF)
-    table1 = far_t[1].reshape(nlon * nlat, HALF)
+    start3(0, group)
+    lax.fori_loop(0, half_line, wait_other, 0)
+    place_rows(other)
+    start2(1, other)
+    hand_on(0, group)
+    start3(1, other)
+    wait4(0, group)
+
+    def far_base(i, carry):
+        edges = pl.ds(pl.multiple_of(i * TILE, TILE), TILE)
+        mbase[edges, :] += far_part(group, edges)
+        return carry
+
+    lax.fori_loop(0, MESH_EDGES // TILE, far_base, 0)
+    hand_on(1, other)
+    wait4(1, other)
 
     def mesh_edges(i, carry):
         edges = pl.ds(pl.multiple_of(i * TILE, TILE), TILE)
-        far = jnp.concatenate([dot(far_hot0[edges, :], table0), dot(far_hot1[edges, :], table1)], axis=1)
-        hidden = silu(mbase[edges, :] + far).astype(BF16)
+        hidden = silu(mbase[edges, :] + far_part(other, edges)).astype(BF16)
         message = layer_norm(dot(hidden, po_v[...])).astype(BF16)
         minflow[...] += dot(minc[:, edges], message)
         return carry
@@ -392,55 +502,62 @@
     update = layer_norm(dot(hidden, pf_v[...]))
     out_ref[0, 0] = (encoded.astype(F32) + update).astype(BF16)
 
-    for copy in halo_copies:
-        copy.wait_send()
-    for copy in near_copies:
-        copy.wait_send()
-
-    def end_line(k, carry):
-        line_copy(k).wait_send()
-        return carry
-
-    lax.fori_loop(1, nlat, end_line, 0)
-    for k in range(1, nx):
-        stage2(k, first).wait_send()
-        stage3(k, second).wait_send()
-    for k in range(nx):
-        stage4(core, k).wait_send()
+    for copy, (*_, step) in zip(halo_copies, halo_moves):
+        guarded(sends(step), copy.wait_send)
+    for copy, (*_, step) in zip(near_copies, near_moves):
+        guarded(sends(step), copy.wait_send)
+
+    def end_mate(k, carry):
+        line_copy(group_mate(k)).wait_send()
+        return carry
+
+    def end_other(k, carry):
+        line_copy(other * half_line + k).wait_send()
+        return carry
+
+    lax.fori_loop(1, half_line, end_mate, 0)
+    lax.fori_loop(0, half_line, end_other, 0)
+    for turn, which in ((0, group), (1, other)):
+        for k in range(1, nx):
+            stage2(turn, which, k, first).wait_send()
+            stage3(turn, which, k, second).wait_send()
+        for k in range(nx):
+            stage4(turn, which, core, k).wait_send()
 
 
 def body(nx, ny, nlat, *args):
     weight = pltpu.VMEM((LATENT, LATENT), BF16)
     narrow = pltpu.VMEM((4, LATENT), BF16)
-    far = nx * ny * nlat
+    half_line = nlat // 2
+    sectors = nx * ny * half_line
     dma = pltpu.SemaphoreType.DMA
     scratch = [
         pltpu.VMEM((GRID_LAT, GRID_LON, LATENT), BF16), pltpu.VMEM((SLOTS, LATENT), BF16),
         pltpu.VMEM((1, GRID_EDGES), I32), pltpu.VMEM((1, GRID_EDGES), I32), pltpu.VMEM((4, GRID_EDGES), BF16),
         pltpu.VMEM((1, MESH_EDGES), I32), pltpu.VMEM((1, MESH_EDGES), I32), pltpu.VMEM((4, MESH_EDGES), BF16),
-        pltpu.VMEM((2, 1, 1), I32),
+        pltpu.VMEM((1, 1, 2), I32),
         weight, weight, narrow, weight, weight, weight, weight,
         weight, weight, narrow, weight, weight, weight, weight,
         pltpu.VMEM((OWN, LATENT), BF16), pltpu.VMEM((PACKED, LATENT), BF16), pltpu.VMEM((HALO, LATENT), BF16),
         pltpu.VMEM((128, LATENT), BF16), pltpu.VMEM((GRID_EDGES, 8), F32), pltpu.VMEM((GRID_EDGES, HALO), BF16),
         pltpu.VMEM((GRID_EDGES, LATENT), F32), pltpu.VMEM((SLOTS, GRID_EDGES), BF16), pltpu.VMEM((SLOTS, LATENT), F32),
-        pltpu.VMEM((512, LATENT), BF16), pltpu.VMEM((BLOCK, LATENT), BF16),
+        pltpu.VMEM((512, LATENT), BF16),
         pltpu.VMEM((128, LATENT), BF16), pltpu.VMEM((MESH_EDGES, 8), F32), pltpu.VMEM((MESH_EDGES, 512), BF16),
-        pltpu.VMEM((MESH_EDGES, far), BF16), pltpu.VMEM((MESH_EDGES, far), BF16),
+        pltpu.VMEM((2, 2, MESH_EDGES, sectors), BF16),
         pltpu.VMEM((MESH_EDGES, LATENT), F32), pltpu.VMEM((SLOTS, MESH_EDGES), BF16), pltpu.VMEM((SLOTS, LATENT), F32),
-        pltpu.VMEM((1, LATENT), F32), pltpu.VMEM((nlat, 1, LATENT), F32), pltpu.VMEM((2, nx, nx, nlat, HALF), BF16),
-        dma((23,)), dma((8,)), dma((8,)), dma((8,)), dma((8,)), dma((nlat,)), dma((nlat,)),
-        dma((nx,)), dma((nx,)), dma((nx,)), dma((nx,)), dma((nx,)), dma((nx,)),
+        pltpu.VMEM((1, LATENT), F32), pltpu.VMEM((nlat, 1, LATENT), F32), pltpu.VMEM((2, 2, nx, nx, half_line, HALF), BF16),
+        dma((23,)), pltpu.SemaphoreType.REGULAR, dma((8,)), dma((8,)), dma((4,)), dma((4,)), dma((nlat,)), dma((nlat,)),
+        dma((2, nx)), dma((2, nx)), dma((2, nx)), dma((2, nx)), dma((2, nx)), dma((2, nx)),
     ]
     return pl.pallas_call(
         functools.partial(kernel, nx, ny, nlat),
-        out_shape=jax.ShapeDtypeStruct((1, 1, SLOTS, LATENT), BF16),
+        out_shape=pltpu.VMEM((1, 1, SLOTS, LATENT), BF16),
         in_specs=[pl.BlockSpec(memory_space=pl.ANY)] * 23,
         out_specs=pl.BlockSpec(memory_space=pltpu.VMEM),
         scratch_shapes=scratch,
         compiler_params=pltpu.CompilerParams(collective_id=0, has_side_effects=True, vmem_limit_bytes=60 * 2**20),
         cost_estimate=pl.CostEstimate(flops=3 * 10**9, bytes_accessed=6 * 10**6, transcendentals=10**6),
-    )(*args)
+    )(*args[:8], jnp.transpose(args[8], (1, 2, 0)), *args[9:])
 
 
 def solution(mesh):

time: 60.3 us -> 59.6 us (0.988)
  local copies, waits for them, and re-layouts: 2.69 us -> 0.62 us
  Pallas kernels: 57.4 us -> 58.8 us
    unnamed x2 -> x1, local copies, waits for them, and re-layouts: 2.69 us -> 0.62 us
    pallas_call x1, Pallas kernels: 57.4 us -> 58.8 us  [body(): pl.pallas_call(functools.partial(kernel, nx, ny, nlat), out_shape=pltpu.V...]
where the time goes in v2:
time: 59.6 us; the launch traced here: 59.5 us
  Pallas kernels  58.8 us (99%)
  local copies, waits for them, and re-layouts  0.62 us (1%)
    pallas_call x1, Pallas kernels, body(): pl.pallas_call(functools.partial(kernel, nx, ny, nlat), out_shape=pltpu.V...  58.8 us

profile of v2, /device:TPU:1, one launch (start us, length us, event | category | flops | bytes accessed | tf_op | source)
XLA Modules:
  0.0 59.5 jit_solution(16190107772249004273)
XLA Ops:
  0.0 58.8 %shard_map.217 = bf16[1,1,40,512]{3,2,1,0:T(8,128)(2,1)S(1)} custom-call(bf16[16,32,512]{2,1,0:T(8,128)(2,1)} %refs_0_.1, bf16[1,1,40,512]{3,2,1,0:T(8,128)(2,1)} %refs_1_.1, s32[1,1,1024]{2,1,0:T(1,128)} %refs_2_.1, s32[1,1,1024]{2,1,0:T(1,128)} %refs_3_.1, bf16[1,1,4,1024]{3,2,1,0:T(4,128)(2,1)} %refs_4_.1, s32[1,1,512]{2,1,0:T(1,128)} %refs_5_.1, ...), custom_call_target="tpu_custom_call" | custom-call | flops 3000000000 | bytes 6000000 | tf_op jit(solution)/shard_map/pallas_call | solution.py:552
  58.8 0.6 %copy.25 = bf16[1,1,40,512]{3,2,1,0:T(8,128)(2,1)} copy(bf16[1,1,40,512]{3,2,1,0:T(8,128)(2,1)S(1)} %shard_map.217) | data formatting | bytes 81920

commit v3 on v2

--- a/solution.py
+++ b/solution.py
@@ -89,10 +89,10 @@
         x_v, nodes_v, gs_v, gt_v, gg_v, ms_v, mt_v, mg_v, ec_v,
         es_v, et_v, eg_v, eo_v, ei_v, ein_v, ef_v,
         ps_v, pt_v, pg_v, po_v, pi_v, pin_v, pf_v,
-        own_t, packed, halo_t, tg_t, columns_v, halo_hot, base, inc, inflow,
-        near_t, mtg_t, mcolumns_v, near_hot, far_hot, mbase, minc, minflow,
+        own_t, packed, halo_t, tg_t, columns_v, halo_hot, base, inc,
+        near_t, mtg_t, mcolumns_v, near_hot, far_hot, mbase, minc,
         row_mine, rows_in, far_t,
-        in_sem, late_sem, halo_ss, halo_rs, near_ss, near_rs, s1_ss, s1_rs, s2_ss, s2_rs, s3_ss, s3_rs, s4_ss, s4_rs,
+        in_sem, late_mate, late_other, halo_ss, halo_rs, near_ss, near_rs, s1_ss, s1_rs, s2_ss, s2_rs, s3_ss, s3_rs, s4_ss, s4_rs,
     ) = refs
     nlon, half_line = nx * ny, nlat // 2
     lon, lat = lax.axis_index("lon"), lax.axis_index("lat")
@@ -109,9 +109,10 @@
 
     sources = [
         (grid_hbm, x_v), (es_hbm, es_v),
-        (mesh_hbm.at[0, 0], nodes_v), (gs_hbm.at[0], gs_v), (gt_hbm.at[0], gt_v), (gg_hbm.at[0, 0], gg_v),
-        (ec_hbm, ec_v), (et_hbm, et_v), (eg_hbm, eg_v), (eo_hbm, eo_v), (ei_hbm, ei_v), (ein_hbm, ein_v),
-        (ef_hbm, ef_v), (ps_hbm, ps_v), (ms_hbm.at[0], ms_v), (mt_hbm.at[0], mt_v), (mg_hbm.at[0, 0], mg_v),
+        (et_hbm, et_v), (eg_hbm, eg_v), (mesh_hbm.at[0, 0], nodes_v), (gs_hbm.at[0], gs_v), (gt_hbm.at[0], gt_v),
+        (gg_hbm.at[0, 0], gg_v), (ec_hbm, ec_v), (eo_hbm, eo_v),
+        (ei_hbm, ei_v), (ein_hbm, ein_v), (ef_hbm, ef_v), (ps_hbm, ps_v),
+        (ms_hbm.at[0], ms_v), (mt_hbm.at[0], mt_v), (mg_hbm.at[0, 0], mg_v),
         (pt_hbm, pt_v), (pg_hbm, pg_v), (po_hbm, po_v), (pi_hbm, pi_v), (pin_hbm, pin_v), (pf_hbm, pf_v),
     ]
     loads = [pltpu.make_async_copy(src, dst, in_sem.at[k]) for k, (src, dst) in enumerate(sources)]
@@ -141,9 +142,6 @@
     def second_peer(k):
         return (first * first_step + lax.rem(second + k, nx) * second_step, lat)
 
-    def group_mate(k):
-        return group * half_line + lax.rem(place_in_line + k, half_line)
-
     barrier = pltpu.get_barrier_semaphore()
 
     def greet(device):
@@ -153,16 +151,12 @@
         if step[1] != 0:
             guarded(sends(step), functools.partial(greet, neighbour(step)))
 
-    @pl.when(lat == half_line)
+    @pl.when(has_above)
     def _():
-        greet((lon, half_line - 1))
-
-    def greet_mate(k, carry):
-        greet((lon, group_mate(k)))
-        return carry
-
-    def greet_upper(k, carry):
-        greet((lon, half_line + k))
+        greet((lon, lat - 1))
+
+    def greet_line(k, carry):
+        greet((lon, k))
         return carry
 
     def greet_plane(k, carry):
@@ -170,27 +164,10 @@
         greet(second_peer(k))
         return carry
 
-    lax.fori_loop(1, half_line, greet_mate, 0)
+    lax.fori_loop(lat + 1, nlat, greet_line, 0)
     lax.fori_loop(1, nx, greet_plane, 0)
-
-    @pl.when(group == 0)
-    def _():
-        lax.fori_loop(0, half_line, greet_upper, 0)
-
-    greetings = 2 + 2 * jnp.where(has_above, 1, 0) + 2 * jnp.where(has_below, 1, 0) + 2 * (nx - 1) + half_line - 1
-    greetings = greetings + jnp.where(group == 1, half_line, jnp.where(lat == half_line - 1, 1, 0))
-
-    loads[0].wait()
-    loads[1].wait()
-    for load in loads[2:14]:
-        load.start()
-
-    def project_own(i, carry):
-        rows = x_v[pl.ds(i * (TILE // GRID_LON), TILE // GRID_LON)].reshape(TILE, LATENT)
-        own_t[pl.ds(pl.multiple_of(i * TILE, TILE), TILE), :] = dot(rows, es_v[...]).astype(BF16)
-        return carry
-
-    lax.fori_loop(0, OWN // TILE, project_own, 0)
+    greetings = 2 + 2 * jnp.where(has_above, 1, 0) + 3 * jnp.where(has_below, 1, 0) + 2 * (nx - 1) + lat
+
     place = lax.broadcasted_iota(I32, (PACKED, 128), 0)
     side = jnp.where(place < 48, place, place - 48)
     third = (side * 43) >> 7
@@ -204,6 +181,11 @@
     wanted = jnp.where(place < 96, edge_row, corner_row)
     wanted = jnp.concatenate([wanted] * (OWN // 128), axis=1)
     pick = jnp.where(lax.broadcasted_iota(I32, (PACKED, OWN), 1) == wanted, 1.0, 0.0).astype(BF16)
+    loads[0].wait()
+    loads[1].wait()
+    for load in loads[2:10]:
+        load.start()
+    own_t[...] = dot(x_v[...].reshape(OWN, LATENT), es_v[...]).astype(BF16)
     packed[...] = dot(pick, own_t[...]).astype(BF16)
 
     pl.semaphore_wait(barrier, greetings)
@@ -228,16 +210,19 @@
     for copy, (*_, step) in zip(halo_copies, halo_moves):
         guarded(sends(step), copy.start)
 
-    @pl.when(group == 1)
-    def _():
-        def report(k, carry):
-            pl.semaphore_signal(late_sem, inc=1, device_id=(lon, k), device_id_type=MESH)
-            return carry
-
-        lax.fori_loop(0, half_line, report, 0)
-
-    for load in loads[14:]:
+    for load in loads[10:]:
         load.start()
+
+    def report_mate(k, carry):
+        pl.semaphore_signal(late_mate, inc=1, device_id=(lon, k), device_id_type=MESH)
+        return carry
+
+    def report_other(k, carry):
+        pl.semaphore_signal(late_other, inc=1, device_id=(lon, k), device_id_type=MESH)
+        return carry
+
+    lax.fori_loop(group * half_line, lat, report_mate, 0)
+    lax.fori_loop(0, group * half_line, report_other, 0)
 
     def no_sector(at, rows):
         halo_t[pl.ds(at, rows), :] = jnp.zeros((rows, LATENT), BF16)
@@ -254,7 +239,7 @@
         no_sector(CORNER + 32, 32)
         near_t[pl.ds(6 * BLOCK, 3 * BLOCK), :] = jnp.zeros((3 * BLOCK, LATENT), BF16)
 
-    for load in loads[2:13]:
+    for load in loads[2:10]:
         load.wait()
     halo_t[pl.ds(352, 32), :] = jnp.zeros((32, LATENT), BF16)
     nodes = nodes_v[...]
@@ -280,7 +265,6 @@
         jnp.zeros((1, GRID_EDGES), F32),
     ])
     inc[...] = incidence(targets, ec_v[0, :, 0:1])
-    inflow[...] = jnp.zeros_like(inflow)
 
     def grid_base(i, carry):
         edges = pl.ds(pl.multiple_of(i * TILE, TILE), TILE)
@@ -290,23 +274,19 @@
         halo_hot[edges, :] = one_hot(columns[:, 6:7], HALO)
         return carry
 
-    lax.fori_loop(0, GRID_EDGES // TILE, grid_base, 0)
+    lax.fori_loop(0, GRID_EDGES // TILE, grid_base, 0, unroll=True)
+    for load in loads[10:14]:
+        load.wait()
     self_term = dot(nodes, ei_v[...])
 
     for copy, (*_, step) in zip(halo_copies, halo_moves):
         guarded(receives(step), copy.wait_recv)
 
-    def grid_edges(i, carry):
-        edges = pl.ds(pl.multiple_of(i * TILE, TILE), TILE)
-        hidden = silu(base[edges, :] + dot(halo_hot[edges, :], halo_t[...])).astype(BF16)
-        message = layer_norm(dot(hidden, eo_v[...])).astype(BF16)
-        inflow[...] += dot(inc[:, edges], message)
-        return carry
-
-    lax.fori_loop(0, GRID_EDGES // TILE, grid_edges, 0)
-    hidden = silu(self_term + dot(inflow[...].astype(BF16), ein_v[...])).astype(BF16)
+    hidden = silu(base[...] + dot(halo_hot[...], halo_t[...])).astype(BF16)
+    message = layer_norm(dot(hidden, eo_v[...])).astype(BF16)
+    inflow = dot(inc[...], message).astype(BF16)
+    hidden = silu(self_term + dot(inflow, ein_v[...])).astype(BF16)
     encoded = (nodes.astype(F32) + layer_norm(dot(hidden, ef_v[...]))).astype(BF16)
-    loads[13].wait()
     term = dot(encoded, ps_v[...]).astype(BF16)
 
     row_mine[...] = term.astype(F32)[0:1, :]
@@ -324,19 +304,17 @@
             device_id=(lon, source), device_id_type=MESH,
         )
 
-    def send_mate(k, carry):
-        line_copy(group_mate(k)).start()
-        return carry
-
-    def send_other(k, carry):
-        line_copy(other * half_line + k).start()
-        return carry
-
-    @pl.when(group == 1)
+    def send_row(k, carry):
+        line_copy(k).start()
+        return carry
+
+    lax.fori_loop(0, lat, send_row, 0)
+
+    @pl.when(place_in_line < half_line - 1)
     def _():
-        lax.fori_loop(0, half_line, send_other, 0)
-
-    lax.fori_loop(1, half_line, send_mate, 0)
+        pl.semaphore_wait(late_mate, half_line - 1 - place_in_line)
+
+    lax.fori_loop(lat + 1, (group + 1) * half_line, send_row, 0)
 
     near_t[pl.ds(4 * BLOCK, SLOTS), :] = term
     near_t[pl.ds(4 * BLOCK + SLOTS, BLOCK - SLOTS), :] = jnp.zeros((BLOCK - SLOTS, LATENT), BF16)
@@ -371,19 +349,13 @@
         mg_v[...].astype(F32), near_at.astype(F32), targets.astype(F32), far_at0.astype(F32), far_at1.astype(F32),
     ])
     minc[...] = incidence(targets, ec_v[0, :, 1:2])
-    minflow[...] = jnp.zeros_like(minflow)
-
-    def mesh_hot(i, carry):
-        edges = pl.ds(pl.multiple_of(i * TILE, TILE), TILE)
-        columns = mcolumns_v[edges, :]
-        near_hot[edges, :] = one_hot(columns[:, 4:5], 512)
-        mbase[edges, :] = dot(target_hot(columns), mtg_t[...])
-        for g in range(2):
-            far_hot[0, g, edges, :] = one_hot(columns[:, 6:7] - g * sectors, sectors)
-            far_hot[1, g, edges, :] = one_hot(columns[:, 7:8] - g * sectors, sectors)
-        return carry
-
-    lax.fori_loop(0, MESH_EDGES // TILE, mesh_hot, 0)
+
+    columns = mcolumns_v[...]
+    near_hot[...] = one_hot(columns[:, 4:5], 512)
+    mbase[...] = dot(target_hot(columns), mtg_t[...])
+    for g in range(2):
+        far_hot[0, g] = one_hot(columns[:, 6:7] - g * sectors, sectors)
+        far_hot[1, g] = one_hot(columns[:, 7:8] - g * sectors, sectors)
     mself_term = dot(encoded, pi_v[...])
 
     near_copies[0].wait_recv()
@@ -443,62 +415,41 @@
         for k in range(nx):
             stage4(turn, which, 1 - core, k).wait_recv()
 
-    def far_part(which, edges):
-        parts = [dot(far_hot[h, which, edges, :], far_t[which, h].reshape(sectors, HALF)) for h in range(2)]
+    def far_part(which):
+        parts = [dot(far_hot[h, which], far_t[which, h].reshape(sectors, HALF)) for h in range(2)]
         return jnp.concatenate(parts, axis=1)
 
-    def wait_mate(k, carry):
-        line_arrival(group_mate(k)).wait_recv()
-        return carry
-
-    def wait_other(k, carry):
-        line_arrival(other * half_line + k).wait_recv()
-        return carry
-
-    lax.fori_loop(1, half_line, wait_mate, 0)
+    def wait_row(k, carry):
+        line_arrival(k).wait_recv()
+        return carry
+
+    lax.fori_loop(group * half_line, lat, wait_row, 0)
+    lax.fori_loop(lat + 1, (group + 1) * half_line, wait_row, 0)
     place_rows(group)
     start2(0, group)
 
     @pl.when(group == 0)
     def _():
-        pl.semaphore_wait(late_sem, half_line)
-        lax.fori_loop(0, half_line, send_other, 0)
+        pl.semaphore_wait(late_other, half_line)
+        lax.fori_loop(half_line, nlat, send_row, 0)
 
     for k in (2, 3):
         guarded(receives(near_moves[k][3]), near_copies[k].wait_recv)
-
-    def near_base(i, carry):
-        edges = pl.ds(pl.multiple_of(i * TILE, TILE), TILE)
-        mbase[edges, :] += dot(near_hot[edges, :], near_t[...])
-        return carry
-
-    lax.fori_loop(0, MESH_EDGES // TILE, near_base, 0)
-    start3(0, group)
-    lax.fori_loop(0, half_line, wait_other, 0)
+    mbase[...] += dot(near_hot[...], near_t[...])
+    lax.fori_loop(other * half_line, (other + 1) * half_line, wait_row, 0)
     place_rows(other)
     start2(1, other)
+    start3(0, group)
+    start3(1, other)
     hand_on(0, group)
-    start3(1, other)
     wait4(0, group)
-
-    def far_base(i, carry):
-        edges = pl.ds(pl.multiple_of(i * TILE, TILE), TILE)
-        mbase[edges, :] += far_part(group, edges)
-        return carry
-
-    lax.fori_loop(0, MESH_EDGES // TILE, far_base, 0)
+    mbase[...] += far_part(group)
     hand_on(1, other)
     wait4(1, other)
-
-    def mesh_edges(i, carry):
-        edges = pl.ds(pl.multiple_of(i * TILE, TILE), TILE)
-        hidden = silu(mbase[edges, :] + far_part(other, edges)).astype(BF16)
-        message = layer_norm(dot(hidden, po_v[...])).astype(BF16)
-        minflow[...] += dot(minc[:, edges], message)
-        return carry
-
-    lax.fori_loop(0, MESH_EDGES // TILE, mesh_edges, 0)
-    hidden = silu(mself_term + dot(minflow[...].astype(BF16), pin_v[...])).astype(BF16)
+    hidden = silu(mbase[...] + far_part(other)).astype(BF16)
+    message = layer_norm(dot(hidden, po_v[...])).astype(BF16)
+    minflow = dot(minc[...], message).astype(BF16)
+    hidden = silu(mself_term + dot(minflow, pin_v[...])).astype(BF16)
     update = layer_norm(dot(hidden, pf_v[...]))
     out_ref[0, 0] = (encoded.astype(F32) + update).astype(BF16)
 
@@ -507,16 +458,12 @@
     for copy, (*_, step) in zip(near_copies, near_moves):
         guarded(sends(step), copy.wait_send)
 
-    def end_mate(k, carry):
-        line_copy(group_mate(k)).wait_send()
-        return carry
-
-    def end_other(k, carry):
-        line_copy(other * half_line + k).wait_send()
-        return carry
-
-    lax.fori_loop(1, half_line, end_mate, 0)
-    lax.fori_loop(0, half_line, end_other, 0)
+    def end_row(k, carry):
+        line_copy(k).wait_send()
+        return carry
+
+    lax.fori_loop(0, lat, end_row, 0)
+    lax.fori_loop(lat + 1, nlat, end_row, 0)
     for turn, which in ((0, group), (1, other)):
         for k in range(1, nx):
             stage2(turn, which, k, first).wait_send()
@@ -540,13 +487,13 @@
         weight, weight, narrow, weight, weight, weight, weight,
         pltpu.VMEM((OWN, LATENT), BF16), pltpu.VMEM((PACKED, LATENT), BF16), pltpu.VMEM((HALO, LATENT), BF16),
         pltpu.VMEM((128, LATENT), BF16), pltpu.VMEM((GRID_EDGES, 8), F32), pltpu.VMEM((GRID_EDGES, HALO), BF16),
-        pltpu.VMEM((GRID_EDGES, LATENT), F32), pltpu.VMEM((SLOTS, GRID_EDGES), BF16), pltpu.VMEM((SLOTS, LATENT), F32),
+        pltpu.VMEM((GRID_EDGES, LATENT), F32), pltpu.VMEM((SLOTS, GRID_EDGES), BF16),
         pltpu.VMEM((512, LATENT), BF16),
         pltpu.VMEM((128, LATENT), BF16), pltpu.VMEM((MESH_EDGES, 8), F32), pltpu.VMEM((MESH_EDGES, 512), BF16),
         pltpu.VMEM((2, 2, MESH_EDGES, sectors), BF16),
-        pltpu.VMEM((MESH_EDGES, LATENT), F32), pltpu.VMEM((SLOTS, MESH_EDGES), BF16), pltpu.VMEM((SLOTS, LATENT), F32),
+        pltpu.VMEM((MESH_EDGES, LATENT), F32), pltpu.VMEM((SLOTS, MESH_EDGES), BF16),
         pltpu.VMEM((1, LATENT), F32), pltpu.VMEM((nlat, 1, LATENT), F32), pltpu.VMEM((2, 2, nx, nx, half_line, HALF), BF16),
-        dma((23,)), pltpu.SemaphoreType.REGULAR, dma((8,)), dma((8,)), dma((4,)), dma((4,)), dma((nlat,)), dma((nlat,)),
+        dma((23,)), pltpu.SemaphoreType.REGULAR, pltpu.SemaphoreType.REGULAR, dma((8,)), dma((8,)), dma((4,)), dma((4,)), dma((nlat,)), dma((nlat,)),
         dma((2, nx)), dma((2, nx)), dma((2, nx)), dma((2, nx)), dma((2, nx)), dma((2, nx)),
     ]
     return pl.pallas_call(

time: 59.6 us -> 51.2 us (0.86)
  Pallas kernels: 58.8 us -> 50.4 us
    pallas_call x1, Pallas kernels: 58.8 us -> 50.4 us  [body(): pl.pallas_call(functools.partial(kernel, nx, ny, nlat), out_shape=pltpu.V...]
where the time goes in v3:
time: 51.2 us; the launch traced here: 51 us
  Pallas kernels  50.4 us (98%)
  local copies, waits for them, and re-layouts  0.62 us (1%)
    pallas_call x1, Pallas kernels, body(): pl.pallas_call(functools.partial(kernel, nx, ny, nlat), out_shape=pltpu.V...  50.4 us

profile of v3, /device:TPU:1, one launch (start us, length us, event | category | flops | bytes accessed | tf_op | source)
XLA Modules:
  0.0 51.0 jit_solution(5974943891820920410)
XLA Ops:
  0.0 50.4 %shard_map.217 = bf16[1,1,40,512]{3,2,1,0:T(8,128)(2,1)S(1)} custom-call(bf16[16,32,512]{2,1,0:T(8,128)(2,1)} %refs_0_.1, bf16[1,1,40,512]{3,2,1,0:T(8,128)(2,1)} %refs_1_.1, s32[1,1,1024]{2,1,0:T(1,128)} %refs_2_.1, s32[1,1,1024]{2,1,0:T(1,128)} %refs_3_.1, bf16[1,1,4,1024]{3,2,1,0:T(4,128)(2,1)} %refs_4_.1, s32[1,1,512]{2,1,0:T(1,128)} %refs_5_.1, ...), custom_call_target="tpu_custom_call" | custom-call | flops 3000000000 | bytes 6000000 | tf_op jit(solution)/shard_map/pallas_call | solution.py:499
  50.4 0.6 %copy.25 = bf16[1,1,40,512]{3,2,1,0:T(8,128)(2,1)} copy(bf16[1,1,40,512]{3,2,1,0:T(8,128)(2,1)S(1)} %shard_map.217) | data formatting | bytes 81920

commit v4 on v3

--- a/solution.py
+++ b/solution.py
@@ -89,10 +89,10 @@
         x_v, nodes_v, gs_v, gt_v, gg_v, ms_v, mt_v, mg_v, ec_v,
         es_v, et_v, eg_v, eo_v, ei_v, ein_v, ef_v,
         ps_v, pt_v, pg_v, po_v, pi_v, pin_v, pf_v,
-        own_t, packed, halo_t, tg_t, columns_v, halo_hot, base, inc,
+        own_t, packed, up_v, down_v, side_v, halo_t, tg_t, columns_v, halo_hot, base, inc,
         near_t, mtg_t, mcolumns_v, near_hot, far_hot, mbase, minc,
         row_mine, rows_in, far_t,
-        in_sem, late_mate, late_other, halo_ss, halo_rs, near_ss, near_rs, s1_ss, s1_rs, s2_ss, s2_rs, s3_ss, s3_rs, s4_ss, s4_rs,
+        in_sem, late_mate, late_other, late_plane, halo_ss, halo_rs, near_ss, near_rs, s1_ss, s1_rs, s2_ss, s2_rs, s3_ss, s3_rs, s4_ss, s4_rs,
     ) = refs
     nlon, half_line = nx * ny, nlat // 2
     lon, lat = lax.axis_index("lon"), lax.axis_index("lat")
@@ -159,14 +159,27 @@
         greet((lon, k))
         return carry
 
-    def greet_plane(k, carry):
-        greet(first_peer(k))
-        greet(second_peer(k))
+    def ranked(k):
+        return jnp.where(k < nx // 2, k, nx + nx // 2 - 1 - k)
+
+    def along_x(k):
+        return (ranked(k) * ny + y, lat)
+
+    def along_y(k):
+        return (x * ny + ranked(k), lat)
+
+    def greet_x(k, carry):
+        greet(along_x(k))
+        return carry
+
+    def greet_y(k, carry):
+        greet(along_y(k))
         return carry
 
     lax.fori_loop(lat + 1, nlat, greet_line, 0)
-    lax.fori_loop(1, nx, greet_plane, 0)
-    greetings = 2 + 2 * jnp.where(has_above, 1, 0) + 3 * jnp.where(has_below, 1, 0) + 2 * (nx - 1) + lat
+    lax.fori_loop(ranked(x) + 1, nx, greet_x, 0)
+    lax.fori_loop(ranked(y) + 1, nx, greet_y, 0)
+    greetings = 2 + 2 * jnp.where(has_above, 1, 0) + 3 * jnp.where(has_below, 1, 0) + lat + ranked(x) + ranked(y)
 
     place = lax.broadcasted_iota(I32, (PACKED, 128), 0)
     side = jnp.where(place < 48, place, place - 48)
@@ -182,30 +195,28 @@
     wanted = jnp.concatenate([wanted] * (OWN // 128), axis=1)
     pick = jnp.where(lax.broadcasted_iota(I32, (PACKED, OWN), 1) == wanted, 1.0, 0.0).astype(BF16)
     loads[0].wait()
-    loads[1].wait()
     for load in loads[2:10]:
         load.start()
-    own_t[...] = dot(x_v[...].reshape(OWN, LATENT), es_v[...]).astype(BF16)
-    packed[...] = dot(pick, own_t[...]).astype(BF16)
+    packed[...] = dot(pick, x_v[...].reshape(OWN, LATENT)).astype(BF16)
 
     pl.semaphore_wait(barrier, greetings)
 
     halo_moves = [
-        (packed.at[pl.ds(0, 48)], LEFT, 48, (0, 1)),
-        (packed.at[pl.ds(48, 48)], RIGHT, 48, (0, -1)),
-        (own_t.at[pl.ds(OWN - 96, 96)], UP, 96, (1, 0)),
-        (own_t.at[pl.ds(0, 96)], DOWN, 96, (-1, 0)),
-        (packed.at[pl.ds(96, 16)], CORNER, 16, (1, 1)),
-        (packed.at[pl.ds(112, 16)], CORNER + 16, 16, (1, -1)),
-        (packed.at[pl.ds(128, 16)], CORNER + 32, 16, (-1, 1)),
-        (packed.at[pl.ds(144, 16)], CORNER + 48, 16, (-1, -1)),
+        (packed.at[pl.ds(0, 48)], side_v.at[pl.ds(0, 48)], (0, 1)),
+        (packed.at[pl.ds(48, 48)], side_v.at[pl.ds(48, 48)], (0, -1)),
+        (x_v.at[pl.ds(GRID_LAT - RIM, RIM)], up_v, (1, 0)),
+        (x_v.at[pl.ds(0, RIM)], down_v, (-1, 0)),
+        (packed.at[pl.ds(96, 16)], side_v.at[pl.ds(96, 16)], (1, 1)),
+        (packed.at[pl.ds(112, 16)], side_v.at[pl.ds(112, 16)], (1, -1)),
+        (packed.at[pl.ds(128, 16)], side_v.at[pl.ds(128, 16)], (-1, 1)),
+        (packed.at[pl.ds(144, 16)], side_v.at[pl.ds(144, 16)], (-1, -1)),
     ]
     halo_copies = [
         pltpu.make_async_remote_copy(
-            src_ref=src, dst_ref=halo_t.at[pl.ds(at, rows)], send_sem=halo_ss.at[k], recv_sem=halo_rs.at[k],
+            src_ref=src, dst_ref=dst, send_sem=halo_ss.at[k], recv_sem=halo_rs.at[k],
             device_id=neighbour(step), device_id_type=MESH,
         )
-        for k, (src, at, rows, step) in enumerate(halo_moves)
+        for k, (src, dst, step) in enumerate(halo_moves)
     ]
     for copy, (*_, step) in zip(halo_copies, halo_moves):
         guarded(sends(step), copy.start)
@@ -221,27 +232,38 @@
         pl.semaphore_signal(late_other, inc=1, device_id=(lon, k), device_id_type=MESH)
         return carry
 
+    def report_x(k, carry):
+        pl.semaphore_signal(late_plane, inc=1, device_id=along_x(k), device_id_type=MESH)
+        return carry
+
+    def report_y(k, carry):
+        pl.semaphore_signal(late_plane, inc=1, device_id=along_y(k), device_id_type=MESH)
+        return carry
+
+    lax.fori_loop(0, ranked(x), report_x, 0)
+    lax.fori_loop(0, ranked(y), report_y, 0)
     lax.fori_loop(group * half_line, lat, report_mate, 0)
     lax.fori_loop(0, group * half_line, report_other, 0)
 
-    def no_sector(at, rows):
-        halo_t[pl.ds(at, rows), :] = jnp.zeros((rows, LATENT), BF16)
+    side_v[pl.ds(PACKED, 32), :] = jnp.zeros((32, LATENT), BF16)
 
     @pl.when(lat == 0)
     def _():
-        no_sector(UP, 96)
-        no_sector(CORNER, 32)
+        up_v[...] = jnp.zeros_like(up_v)
+        side_v[pl.ds(96, 32), :] = jnp.zeros((32, LATENT), BF16)
         near_t[pl.ds(0, 3 * BLOCK), :] = jnp.zeros((3 * BLOCK, LATENT), BF16)
 
     @pl.when(lat == nlat - 1)
     def _():
-        no_sector(DOWN, 96)
-        no_sector(CORNER + 32, 32)
+        down_v[...] = jnp.zeros_like(down_v)
+        side_v[pl.ds(128, 32), :] = jnp.zeros((32, LATENT), BF16)
         near_t[pl.ds(6 * BLOCK, 3 * BLOCK), :] = jnp.zeros((3 * BLOCK, LATENT), BF16)
+
+    loads[1].wait()
+    own_t[...] = dot(x_v[...].reshape(OWN, LATENT), es_v[...]).astype(BF16)
 
     for load in loads[2:10]:
         load.wait()
-    halo_t[pl.ds(352, 32), :] = jnp.zeros((32, LATENT), BF16)
     nodes = nodes_v[...]
     fill_target_table(tg_t, nodes, et_v[...], eg_v[...])
     s = gs_v[...]
@@ -282,6 +304,9 @@
     for copy, (*_, step) in zip(halo_copies, halo_moves):
         guarded(receives(step), copy.wait_recv)
 
+    halo_t[0:96, :] = dot(up_v[...].reshape(96, LATENT), es_v[...]).astype(BF16)
+    halo_t[96:192, :] = dot(down_v[...].reshape(96, LATENT), es_v[...]).astype(BF16)
+    halo_t[192:HALO, :] = dot(side_v[...], es_v[...]).astype(BF16)
     hidden = silu(base[...] + dot(halo_hot[...], halo_t[...])).astype(BF16)
     message = layer_norm(dot(hidden, eo_v[...])).astype(BF16)
     inflow = dot(inc[...], message).astype(BF16)
@@ -335,6 +360,11 @@
     fill_target_table(mtg_t, encoded, pt_v[...], pg_v[...])
     s = ms_v[...]
     sectors = nlon * half_line
+
+    def slot_of(step):
+        step = jnp.where(step < 0, step + nx, step)
+        return jnp.where(step == 0, 0, jnp.where(step <= nx // 2, 2 * step - 1, 2 * (nx - step)))
+
     near = s < 9 * SLOTS
     sector = (s * 1639) >> 16
     near_at = jnp.where(near, sector * BLOCK + (s - sector * SLOTS), -1)
@@ -342,8 +372,8 @@
     plane, line = t // nlat, lax.rem(t, nlat)
     far_x, far_y = plane // ny, lax.rem(plane, ny)
     offset = (line // half_line) * sectors + lax.rem(line, half_line)
-    far_at0 = jnp.where(near, -1, (far_y * nx + far_x) * half_line + offset)
-    far_at1 = jnp.where(near, -1, plane * half_line + offset)
+    far_at0 = jnp.where(near, -1, (far_y * nx + slot_of(far_x - x)) * half_line + offset)
+    far_at1 = jnp.where(near, -1, (far_x * nx + slot_of(far_y - y)) * half_line + offset)
     targets = mt_v[...]
     mcolumns_v[...] = transposed([
         mg_v[...].astype(F32), near_at.astype(F32), targets.astype(F32), far_at0.astype(F32), far_at1.astype(F32),
@@ -369,19 +399,25 @@
         for k in range(half_line):
             block = jnp.where(row_at == k, rows_in[which * half_line + k], block)
         half = jnp.where(core == 0, block[:, :HALF], block[:, HALF:])
-        far_t[which, core, second, first] = half.astype(BF16)
-
-    def stage2(turn, which, k, source):
-        at = far_t.at[which, core, second, source]
+        far_t[which, core, second, 0] = half.astype(BF16)
+
+    def fixed_slot(step):
+        return 0 if step == 0 else 2 * step - 1 if step <= nx // 2 else 2 * (nx - step)
+
+    def stage2(turn, which, k):
+        slot = fixed_slot(nx - k)
         return pltpu.make_async_remote_copy(
-            src_ref=at, dst_ref=at, send_sem=s2_ss.at[turn, k], recv_sem=s2_rs.at[turn, source],
-            device_id=first_peer(k), device_id_type=MESH,
-        )
-
-    def stage3(turn, which, k, source):
-        at = far_t.at[which, core, source]
+            src_ref=far_t.at[which, core, second, 0], dst_ref=far_t.at[which, core, second, slot],
+            send_sem=s2_ss.at[turn, slot], recv_sem=s2_rs.at[turn, slot], device_id=first_peer(k), device_id_type=MESH,
+        )
+
+    parts = [(0, 3), (3, 5), (5, 7), (7, 8)] if nx == 8 else [(0, 1), (1, nx)]
+
+    def stage3(turn, which, part, k, source):
+        low, high = parts[part]
+        at = far_t.at[which, core, source, pl.ds(low, high - low)]
         return pltpu.make_async_remote_copy(
-            src_ref=at, dst_ref=at, send_sem=s3_ss.at[turn, k], recv_sem=s3_rs.at[turn, source],
+            src_ref=at, dst_ref=at, send_sem=s3_ss.at[turn, part, k], recv_sem=s3_rs.at[turn, part, source],
             device_id=second_peer(k), device_id_type=MESH,
         )
 
@@ -396,19 +432,22 @@
 
     def start2(turn, which):
         for k in range(1, nx):
-            stage2(turn, which, k, first).start()
+            stage2(turn, which, k).start()
 
     def start3(turn, which):
-        for k in range(1, nx):
-            stage2(turn, which, k, lax.rem(first + k, nx)).wait_recv()
-        for k in range(1, nx):
-            stage3(turn, which, k, second).start()
+        for part, (low, high) in enumerate(parts):
+            for k in range(1, nx):
+                if low <= fixed_slot(nx - k) < high:
+                    stage2(turn, which, k).wait_recv()
+            for k in reversed(order):
+                stage3(turn, which, part, k, second).start()
         stage4(turn, which, core, second).start()
 
     def hand_on(turn, which):
         for k in order:
             source = lax.rem(second + k, nx)
-            stage3(turn, which, k, source).wait_recv()
+            for part in range(len(parts)):
+                stage3(turn, which, part, k, source).wait_recv()
             stage4(turn, which, core, source).start()
 
     def wait4(turn, which):
@@ -426,6 +465,12 @@
     lax.fori_loop(group * half_line, lat, wait_row, 0)
     lax.fori_loop(lat + 1, (group + 1) * half_line, wait_row, 0)
     place_rows(group)
+    later = 2 * (nx - 1) - ranked(x) - ranked(y)
+
+    @pl.when(later > 0)
+    def _():
+        pl.semaphore_wait(late_plane, later)
+
     start2(0, group)
 
     @pl.when(group == 0)
@@ -433,13 +478,13 @@
         pl.semaphore_wait(late_other, half_line)
         lax.fori_loop(half_line, nlat, send_row, 0)
 
-    for k in (2, 3):
-        guarded(receives(near_moves[k][3]), near_copies[k].wait_recv)
-    mbase[...] += dot(near_hot[...], near_t[...])
     lax.fori_loop(other * half_line, (other + 1) * half_line, wait_row, 0)
     place_rows(other)
     start2(1, other)
     start3(0, group)
+    for k in (2, 3):
+        guarded(receives(near_moves[k][3]), near_copies[k].wait_recv)
+    mbase[...] += dot(near_hot[...], near_t[...])
     start3(1, other)
     hand_on(0, group)
     wait4(0, group)
@@ -466,8 +511,9 @@
     lax.fori_loop(lat + 1, nlat, end_row, 0)
     for turn, which in ((0, group), (1, other)):
         for k in range(1, nx):
-            stage2(turn, which, k, first).wait_send()
-            stage3(turn, which, k, second).wait_send()
+            stage2(turn, which, k).wait_send()
+            for part in range(len(parts)):
+                stage3(turn, which, part, k, second).wait_send()
         for k in range(nx):
             stage4(turn, which, core, k).wait_send()
 
@@ -485,7 +531,8 @@
         pltpu.VMEM((1, 1, 2), I32),
         weight, weight, narrow, weight, weight, weight, weight,
         weight, weight, narrow, weight, weight, weight, weight,
-        pltpu.VMEM((OWN, LATENT), BF16), pltpu.VMEM((PACKED, LATENT), BF16), pltpu.VMEM((HALO, LATENT), BF16),
+        pltpu.VMEM((OWN, LATENT), BF16), pltpu.VMEM((PACKED, LATENT), BF16), pltpu.VMEM((RIM, GRID_LON, LATENT), BF16),
+        pltpu.VMEM((RIM, GRID_LON, LATENT), BF16), pltpu.VMEM((PACKED + 32, LATENT), BF16), pltpu.VMEM((HALO, LATENT), BF16),
         pltpu.VMEM((128, LATENT), BF16), pltpu.VMEM((GRID_EDGES, 8), F32), pltpu.VMEM((GRID_EDGES, HALO), BF16),
         pltpu.VMEM((GRID_EDGES, LATENT), F32), pltpu.VMEM((SLOTS, GRID_EDGES), BF16),
         pltpu.VMEM((512, LATENT), BF16),
@@ -493,8 +540,8 @@
         pltpu.VMEM((2, 2, MESH_EDGES, sectors), BF16),
         pltpu.VMEM((MESH_EDGES, LATENT), F32), pltpu.VMEM((SLOTS, MESH_EDGES), BF16),
         pltpu.VMEM((1, LATENT), F32), pltpu.VMEM((nlat, 1, LATENT), F32), pltpu.VMEM((2, 2, nx, nx, half_line, HALF), BF16),
-        dma((23,)), pltpu.SemaphoreType.REGULAR, pltpu.SemaphoreType.REGULAR, dma((8,)), dma((8,)), dma((4,)), dma((4,)), dma((nlat,)), dma((nlat,)),
-        dma((2, nx)), dma((2, nx)), dma((2, nx)), dma((2, nx)), dma((2, nx)), dma((2, nx)),
+        dma((23,)), pltpu.SemaphoreType.REGULAR, pltpu.SemaphoreType.REGULAR, pltpu.SemaphoreType.REGULAR, dma((8,)), dma((8,)), dma((4,)), dma((4,)), dma((nlat,)), dma((nlat,)),
+        dma((2, nx)), dma((2, nx)), dma((2, 4, nx)), dma((2, 4, nx)), dma((2, nx)), dma((2, nx)),
     ]
     return pl.pallas_call(
         functools.partial(kernel, nx, ny, nlat),

time: 51.2 us -> 49.7 us (0.971)
  Pallas kernels: 50.4 us -> 48.9 us
    pallas_call x1, Pallas kernels: 50.4 us -> 48.9 us  [body(): pl.pallas_call(functools.partial(kernel, nx, ny, nlat), out_shape=pltpu.V...]
where the time goes in v4:
time: 49.7 us; the launch traced here: 49.5 us
  Pallas kernels  48.9 us (98%)
  local copies, waits for them, and re-layouts  0.62 us (1%)
    pallas_call x1, Pallas kernels, body(): pl.pallas_call(functools.partial(kernel, nx, ny, nlat), out_shape=pltpu.V...  48.9 us

profile of v4, /device:TPU:1, one launch (start us, length us, event | category | flops | bytes accessed | tf_op | source)
XLA Modules:
  0.0 49.5 jit_solution(7975801182679132719)
XLA Ops:
  0.0 48.9 %shard_map.217 = bf16[1,1,40,512]{3,2,1,0:T(8,128)(2,1)S(1)} custom-call(bf16[16,32,512]{2,1,0:T(8,128)(2,1)} %refs_0_.1, bf16[1,1,40,512]{3,2,1,0:T(8,128)(2,1)} %refs_1_.1, s32[1,1,1024]{2,1,0:T(1,128)} %refs_2_.1, s32[1,1,1024]{2,1,0:T(1,128)} %refs_3_.1, bf16[1,1,4,1024]{3,2,1,0:T(4,128)(2,1)} %refs_4_.1, s32[1,1,512]{2,1,0:T(1,128)} %refs_5_.1, ...), custom_call_target="tpu_custom_call" | custom-call | flops 3000000000 | bytes 6000000 | tf_op jit(solution)/shard_map/pallas_call | solution.py:546
  48.9 0.6 %copy.25 = bf16[1,1,40,512]{3,2,1,0:T(8,128)(2,1)} copy(bf16[1,1,40,512]{3,2,1,0:T(8,128)(2,1)S(1)} %shard_map.217) | data formatting | bytes 81920

commit v5 on v4

--- a/solution.py
+++ b/solution.py
@@ -122,7 +122,7 @@
     around = [(0, 1), (0, -1), (1, 0), (-1, 0), (1, 1), (1, -1), (-1, 1), (-1, -1)]
 
     def neighbour(step):
-        return (lax.rem(lon + step[1] + nlon, nlon), lat + step[0])
+        return (lax.rem(lon + step[1] + nlon, nlon), lax.rem(lat + step[0] + nlat, nlat))
 
     def receives(step):
         return {0: None, 1: has_above, -1: has_below}[step[0]]

time: 49.7 us -> 49.7 us (level)
  no operation moved by 1% of the time
where the time goes in v5:
time: 49.7 us; the launch traced here: 49.5 us
  Pallas kernels  48.9 us (98%)
  local copies, waits for them, and re-layouts  0.62 us (1%)
    pallas_call x1, Pallas kernels, body(): pl.pallas_call(functools.partial(kernel, nx, ny, nlat), out_shape=pltpu.V...  48.9 us

profile of v5, /device:TPU:1, one launch (start us, length us, event | category | flops | bytes accessed | tf_op | source)
XLA Modules:
  0.0 49.5 jit_solution(12804770661216544416)
XLA Ops:
  0.0 48.9 %shard_map.217 = bf16[1,1,40,512]{3,2,1,0:T(8,128)(2,1)S(1)} custom-call(bf16[16,32,512]{2,1,0:T(8,128)(2,1)} %refs_0_.1, bf16[1,1,40,512]{3,2,1,0:T(8,128)(2,1)} %refs_1_.1, s32[1,1,1024]{2,1,0:T(1,128)} %refs_2_.1, s32[1,1,1024]{2,1,0:T(1,128)} %refs_3_.1, bf16[1,1,4,1024]{3,2,1,0:T(4,128)(2,1)} %refs_4_.1, s32[1,1,512]{2,1,0:T(1,128)} %refs_5_.1, ...), custom_call_target="tpu_custom_call" | custom-call | flops 3000000000 | bytes 6000000 | tf_op jit(solution)/shard_map/pallas_call | solution.py:546
  48.9 0.6 %copy.25 = bf16[1,1,40,512]{3,2,1,0:T(8,128)(2,1)} copy(bf16[1,1,40,512]{3,2,1,0:T(8,128)(2,1)S(1)} %shard_map.217) | data formatting | bytes 81920
